TPU v7x, 32 devices: a whole 2x2x4 slice. The times are simulated.
32 devices in a mesh: ao: 8 (over z, core), chol: 4 (over y, x).
Axes of the slice: x: 2, y: 2, z: 4, core: 2. Of those that a mesh axis runs over, the one named last changes fastest.
Arguments:
- cholesky: bfloat16 [8, 3072, 3072], P('chol', 'ao'), may hold values from -2.109375 to 2.109375
- coeffs: bfloat16 [3072, 128], P('ao'), may hold values from -0.109375 to 0.109375
Outputs:
- pair_integrals: bfloat16 [16384, 16384], P('ao', 'chol')
All inputs are finite; a program needn't handle non-finite values.
Results may differ from a plain program's by a relative error of at most 0.007.
Values may be sent and summed in bfloat16 or wider, within the bound.
No kernel may reach another device: no remote copies, remote signals or barrier semaphores. Data moves between devices by JAX's collectives and lax.ppermute only.
A program may use at most 64 MiB of HBM per device.

v0:
```python
import jax
import jax.numpy as jnp
from jax import lax
from jax.sharding import PartitionSpec as P


def body(cholesky, coeffs):
    vec_dev = cholesky.shape[0]
    orbitals = coeffs.shape[1]
    projected = jnp.einsum(
        "prk,kj->prj",
        cholesky,
        lax.all_gather(coeffs, "ao", axis=0, tiled=True),
        preferred_element_type=jnp.float32,
    ).astype(jnp.bfloat16)
    partial_value = jnp.einsum("ri,prj->pij", coeffs, projected, preferred_element_type=jnp.float32)
    partial_value = partial_value.reshape(vec_dev, orbitals * orbitals)
    pair_values = lax.psum(partial_value, "ao").astype(jnp.bfloat16)
    pair_count = orbitals * orbitals
    row_count = pair_count // lax.axis_size("ao")
    col_count = pair_count // lax.axis_size("chol")
    row_offset = lax.axis_index("ao") * row_count
    col_offset = lax.axis_index("chol") * col_count
    segment = lax.all_gather(pair_values, "chol", axis=0, tiled=True)
    row_part = lax.dynamic_slice_in_dim(segment, row_offset, row_count, 1)
    col_part = lax.dynamic_slice_in_dim(segment, col_offset, col_count, 1)
    result_block = jnp.einsum("pa,pb->ab", row_part, col_part, preferred_element_type=jnp.float32)
    return result_block.astype(jnp.bfloat16)


def solution(mesh):
    placed = (P("chol", "ao", None), P("ao", None))
    return jax.shard_map(
        body, mesh=mesh, in_specs=placed, out_specs=P("ao", "chol"), check_vma=False
    )
```

profile of v0, /device:TPU:0, one launch (start us, length us, event | category | flops | bytes accessed | tf_op | source)
XLA Modules:
  0.0 69.8 jit_solution(18071074608802039835)
XLA Ops:
  0.0 17.4 %all_gather.6 = bf16[3072,128]{1,0:T(8,128)(2,1)S(1)} all-gather(bf16[384,128]{1,0:T(8,128)(2,1)} %param.3), channel_id=1, replica_groups=mesh['ao'=8,'chol'=4] {'ao'}, dimensions={0}, use_global_device_ids=true | all-gather | bytes 884736 | tf_op jit(solution)/shard_map/all_gather | solution.py:13
  17.4 4.0 %fusion.1 = f32[2,128,128]{1,2,0:T(8,128)S(1)} fusion(bf16[2,384,3072]{2,1,0:T(8,128)(2,1)} %param.2, bf16[3072,128]{1,0:T(8,128)(2,1)S(1)} %all_gather.6, bf16[384,128]{1,0:T(8,128)(2,1)} %param.3), kind=kOutput, calls=%fused_computation.3 | convolution fusion | flops 629243904 | bytes 5734400 | tf_op jit(solution)/shard_map/ri,prj->pij/dot_general | solution.py:16
  21.4 0.1 copy.5
  21.5 0.1 copy.9
  21.6 30.5 %all-reduce.1 = bf16[2,16384]{1,0:T(2,128)(2,1)S(1)} all-reduce(f32[2,16384]{1,0:T(2,128)S(1)} %bitcast.18), channel_id=1, replica_groups=mesh['ao'=8,'chol'=4] {'ao'}, use_global_device_ids=true, to_apply=%region_0.0 | all-reduce | flops 32768 | bytes 196608 | tf_op jit(solution)/shard_map/psum | solution.py:18
  52.1 9.0 %all-gather = bf16[4,2,16384]{2,1,0:T(2,128)(2,1)S(1)} all-gather(bf16[1,2,16384]{2,1,0:T(2,128)(2,1)S(1)} %bitcast.19), channel_id=1, replica_groups=mesh['ao'=8,'chol'=4] {'chol'}, dimensions={0}, use_global_device_ids=true | all-gather | bytes 327680 | tf_op jit(solution)/shard_map/all_gather | solution.py:24
  61.1 0.1 reshape.5
  61.2 8.6 %convolution_convert_fusion = bf16[2048,4096]{1,0:T(8,128)(2,1)} fusion(bf16[8,16384]{1,0:T(8,128)(2,1)S(1)} %reshape.5, s32[]{:T(128)S(6)} %select_n.7, s32[]{:T(128)S(6)} %select_n.6), kind=kOutput, calls=%fused_computation | convolution fusion | flops 142606336 | bytes 16875528 | tf_op jit(solution)/shard_map/pa,pb->ab/dot_general | solution.py:27
where the time goes:
time: 70 us; the launch traced here: 69.8 us
  blocking collectives  56.9 us (81%)
  matrix products  12.5 us (18%)
    psum x1, blocking collectives, body(): pair_values = lax.psum(partial_value, 'ao').astype(jnp.bfloat16)  30.5 us
    all_gather x1, blocking collectives, body(): lax.all_gather(coeffs, 'ao', axis=0, tiled=True)  17.4 us
    all_gather x1, blocking collectives, body(): segment = lax.all_gather(pair_values, 'chol', axis=0, tiled=True)  9 us
    dot_general x1, matrix products, body(): jnp.einsum('pa,pb->ab', row_part, col_part, preferred_element_type=jnp.fl...  8.56 us
    dot_general x1, matrix products, body(): jnp.einsum('ri,prj->pij', coeffs, projected, preferred_element_type=jnp.f...  3.97 us

commit v1 on v0

v1 whole, which is shorter than its diff:
```python
import functools

import jax
import jax.numpy as jnp
from jax import lax
from jax.experimental import pallas as pl
from jax.experimental.pallas import tpu as pltpu
from jax.sharding import Mesh, PartitionSpec as P

CORES = 2
AO = ("z", "core")
SWAP = [(0, 1), (1, 0)]


def pick(array, index, size, dim):
    return lax.dynamic_slice_in_dim(array, index * size, size, dim)


def flip(array, axis, step):
    count = lax.axis_size(axis)
    return lax.ppermute(array, axis, [(d, d ^ step) for d in range(count)])


def project_kernel(nz, left_ref, *refs):
    held, out_ref = refs[:nz], refs[-1]
    z, core = lax.axis_index("z"), lax.axis_index("core")
    for p in range(out_ref.shape[0]):
        total = refs[nz][p] if len(refs) > nz + 1 else 0.0
        for s in range(nz):
            total += lax.dot_general(
                left_ref[p, z ^ s, core if left_ref.shape[2] > 1 else 0],
                held[s][...],
                (((0,), (0,)), ((), ())),
                preferred_element_type=jnp.float32,
            )
        out_ref[p] = total


def project(left, held, *before, flops):
    vec_dev, nz, _, rows, orbitals = left.shape
    whole = pl.BlockSpec(memory_space=pltpu.VMEM)
    return pl.pallas_call(
        functools.partial(project_kernel, nz),
        out_shape=jax.ShapeDtypeStruct((vec_dev, orbitals, orbitals), jnp.float32),
        in_specs=[whole] * (1 + nz + len(before)),
        out_specs=whole,
        compiler_params=pltpu.CompilerParams(vmem_limit_bytes=32 << 20),
        cost_estimate=pl.CostEstimate(
            flops=flops, bytes_accessed=flops // 1000, transcendentals=0
        ),
    )(left, *held, *before)


def head_kernel(slab, row_ref, col_ref, head_ref, flipped_ref):
    flipped_ref[...] = row_ref[...].astype(jnp.float32).T.astype(flipped_ref.dtype)
    for n in range(head_ref.shape[1] // slab):
        at = pl.ds(n * slab, slab)
        head_ref[:, at] = jnp.dot(
            flipped_ref[...], col_ref[:, at], preferred_element_type=jnp.float32
        ).astype(head_ref.dtype)


def rest_kernel(slab, side, head_ref, flipped_ref, col_ref, out_ref, block, sems):
    heads = head_ref.shape[1] // slab
    own, per = sems.shape[0] // CORES, side // slab
    core = lax.axis_index("core")

    def write(source, n, t):
        s, owner = t % own, (core + t // own) % CORES
        to = (s // per * CORES + owner) * side + s % per * slab
        return pltpu.make_async_copy(
            source.at[:, pl.ds(pl.multiple_of(n * slab, slab), slab)],
            out_ref.at[:, pl.ds(pl.multiple_of(to, slab), slab)],
            sems.at[t],
        )

    for n in range(heads):
        write(head_ref, n, n).start()

    rest = sems.shape[0] - heads

    @pl.loop(0, rest, unroll=3 if rest % 3 == 0 else 1)
    def _(n):
        at = pl.ds(pl.multiple_of(n * slab, slab), slab)
        block[:, at] = jnp.dot(
            flipped_ref[...], col_ref[:, at], preferred_element_type=jnp.float32
        ).astype(block.dtype)
        write(block, n, n + heads).start()

    for n in range(heads):
        write(head_ref, n, n).wait()

    @pl.loop(0, rest)
    def _(n):
        write(block, n, n + heads).wait()


def head_product(row_part, col_part, slab):
    vecs, rows = row_part.shape
    width = slab * max(1, col_part.shape[1] // slab // 2)
    whole = pl.BlockSpec(memory_space=pltpu.VMEM)
    return pl.pallas_call(
        functools.partial(head_kernel, slab),
        out_shape=(
            jax.ShapeDtypeStruct((rows, width), jnp.bfloat16),
            jax.ShapeDtypeStruct((rows, vecs), jnp.bfloat16),
        ),
        in_specs=[whole] * 2,
        out_specs=(whole, whole),
        compiler_params=pltpu.CompilerParams(vmem_limit_bytes=24 << 20),
        cost_estimate=pl.CostEstimate(
            flops=2 * vecs * rows * width, bytes_accessed=2 * rows * width, transcendentals=0
        ),
    )(row_part, col_part)


def rest_product(head, flipped, col_rest, side, slab):
    rows, vecs = flipped.shape
    width = col_rest.shape[1]
    cols = head.shape[1] + width
    whole = pl.BlockSpec(memory_space=pltpu.VMEM)
    return pl.pallas_call(
        functools.partial(rest_kernel, slab, side),
        out_shape=jax.ShapeDtypeStruct((rows, cols), jnp.bfloat16),
        in_specs=[whole] * 3,
        out_specs=pl.BlockSpec(memory_space=pl.ANY),
        scratch_shapes=[
            pltpu.VMEM((rows, width), jnp.bfloat16),
            pltpu.SemaphoreType.DMA((cols // slab,)),
        ],
        compiler_params=pltpu.CompilerParams(vmem_limit_bytes=32 << 20),
        cost_estimate=pl.CostEstimate(
            flops=2 * vecs * rows * width, bytes_accessed=2 * rows * cols, transcendentals=0
        ),
    )(head, flipped, col_rest)


def body(cholesky, coeffs):
    vec_dev, rows, nao = cholesky.shape
    orbitals = coeffs.shape[1]
    nz, n_chol = lax.axis_size("z"), lax.axis_size("chol")
    z, core, chol = lax.axis_index("z"), lax.axis_index("core"), lax.axis_index("chol")

    held = [coeffs] + [flip(coeffs, "z", s) for s in range(1, nz)]

    left = jnp.einsum("ri,prk->pki", coeffs, cholesky, preferred_element_type=jnp.float32)
    left = left.astype(jnp.bfloat16).reshape(vec_dev, nz, CORES, rows, orbitals)
    give = lax.dynamic_slice_in_dim(left, 1 - core, 1, 2)
    got = lax.ppermute(give, "core", SWAP)
    partial = project(left, held, flops=10**11)
    partial = project(got, held, partial, flops=2 * got.size * orbitals)

    span = orbitals // (nz * CORES)
    partial = partial.reshape(vec_dev, nz, CORES, span, orbitals)
    total = lax.dynamic_index_in_dim(partial, core, 2, keepdims=False)
    total += lax.ppermute(
        lax.dynamic_index_in_dim(partial, 1 - core, 2, keepdims=False), "core", SWAP
    )
    rounded = total.astype(jnp.bfloat16)
    for s in range(1, nz):
        total += flip(rounded, "z", s).astype(jnp.float32)
    values = total.astype(jnp.bfloat16)

    wide = nz // n_chol
    row_out = pick(values, z, 1, 1)
    seen = [jnp.concatenate([row_out, pick(values, chol, wide, 1)], 1)]
    for s in range(n_chol - 1, 0, -1):
        seen.append(flip(jnp.concatenate([row_out, pick(values, chol ^ s, wide, 1)], 1), "chol", s))
    seen = jnp.concatenate(seen, 0)
    vecs = seen.shape[0]
    row_part, col_own = seen[:, :1].reshape(vecs, -1), seen[:, 1:].reshape(vecs, -1)

    col_got = lax.ppermute(seen[:, 1:], "core", SWAP).reshape(vecs, -1)
    side = span * orbitals
    slab = min(side, 512)
    head, flipped = head_product(row_part, col_own, slab)
    col_rest = jnp.concatenate([col_own[:, head.shape[1] :], col_got], 1)
    return rest_product(head, flipped, col_rest, side, slab)


def solution(mesh):
    n_ao, n_chol = mesh.shape["ao"], mesh.shape["chol"]
    split = Mesh(mesh.devices.reshape(n_ao // CORES, CORES, n_chol), (*AO, "chol"))
    placed = (P("chol", AO, None), P(AO, None))
    return jax.shard_map(
        body, mesh=split, in_specs=placed, out_specs=P(AO, "chol"), check_vma=False
    )
```

time: 70 us -> 37.9 us (0.54)
  blocking collectives: 56.9 us -> 0 us
  starting transfers between devices: 0 us -> 13.9 us
  waiting for transfers between devices: 0 us -> 11.3 us
  matrix products: 12.5 us -> 3.77 us
  Pallas kernels: 0 us -> 8.08 us
    psum x1 -> x0, blocking collectives: 30.5 us -> none  [body(): pair_values = lax.psum(partial_value, 'ao').astype(jnp.bfloat16)]
    all_gather x2 -> x0, blocking collectives: 26.4 us -> none  [the longest x1 17.4 us: body(): lax.all_gather(coeffs, 'ao', axis=0, tiled=True)]
    ppermute x0 -> x12, starting transfers between devices: none -> 13.9 us  [the longest x9 13.7 us: flip(): return lax.ppermute(array, axis, [(d, d ^ step) for d in range(count)])]
    ppermute x0 -> x12, waiting for transfers between devices: none -> 11.3 us  [the longest x9 10.1 us: flip(): return lax.ppermute(array, axis, [(d, d ^ step) for d in range(count)])]
    dot_general x2 -> x1, matrix products: 12.5 us -> 3.77 us  [body(): jnp.einsum('ri,prk->pki', coeffs, cholesky, preferred_element_type=jnp.fl...]
    pallas_call x0 -> x4, Pallas kernels: none -> 8.08 us  [the longest x1 5.94 us: rest_product(): pl.pallas_call(functools.partial(rest_kernel, slab, side), out_shape=jax....]
  transfers between devices with their start and end apart: 0 -> 12, of which waited for: 0 -> 7; matrix products, arithmetic and copies ran while one was open for 0% -> 10% of each run, Pallas kernels for 0% -> 5%
where the time goes in v1:
time: 37.9 us; the launch traced here: 37.7 us
  starting transfers between devices  13.9 us (37%)
  waiting for transfers between devices  11.3 us (30%)
  Pallas kernels  8.08 us (21%)
  matrix products  3.77 us (10%)
    ppermute x9, starting transfers between devices, flip(): return lax.ppermute(array, axis, [(d, d ^ step) for d in range(count)])  13.7 us
    ppermute x9, waiting for transfers between devices, flip(): return lax.ppermute(array, axis, [(d, d ^ step) for d in range(count)])  10.1 us
    pallas_call x1, Pallas kernels, rest_product(): pl.pallas_call(functools.partial(rest_kernel, slab, side), out_shape=jax....  5.94 us
    dot_general x1, matrix products, body(): jnp.einsum('ri,prk->pki', coeffs, cholesky, preferred_element_type=jnp.fl...  3.77 us
    pallas_call x1, Pallas kernels, head_product(): pl.pallas_call(functools.partial(head_kernel, slab), out_shape=(jax.Shape...  1.31 us
    ppermute x1, waiting for transfers between devices, body(): lax.ppermute(lax.dynamic_index_in_dim(partial, 1 - core, 2, keepdims=Fals...  1.24 us
    pallas_call x2, Pallas kernels, project(): pl.pallas_call(functools.partial(project_kernel, nz), out_shape=jax.Shape...  0.83 us
  transfers between devices with their start and end apart: 12, of which 7 were waited for; matrix products, arithmetic and copies ran while one was open for 10% of the time, Pallas kernels for 5%

profile of v1, /device:TPU:0, one launch (start us, length us, event | category | flops | bytes accessed | tf_op | source)
XLA Modules:
  0.0 37.7 jit_solution(6018621856854413123)
XLA Ops:
  0.0 0.0 copy-start
  0.0 5.0 %collective-permute-start.3 = (bf16[384,128]{1,0:T(8,128)(2,1)}, bf16[384,128]{1,0:T(8,128)(2,1)S(1)}, u32[]{:S(2)}, u32[]{:S(2)}) collective-permute-start(bf16[384,128]{1,0:T(8,128)(2,1)} %refs_0_.3), channel_id=1, source_target_pairs={{0,24},{8,16},{16,8},{24,0},{1,25},{9,17},{17,9},{25,1},{2,26},{10... | collective-permute-start | bytes 294920 | tf_op jit(solution)/shard_map/ppermute | solution.py:21
  5.1 0.0 collective-permute-start.2
  5.1 0.6 %collective-permute-start.1 = (bf16[384,128]{1,0:T(8,128)(2,1)}, bf16[384,128]{1,0:T(8,128)(2,1)S(1)}, u32[]{:S(2)}, u32[]{:S(2)}) collective-permute-start(bf16[384,128]{1,0:T(8,128)(2,1)} %refs_0_.3), channel_id=1, source_target_pairs={{0,8},{8,0},{16,24},{24,16},{1,9},{9,1},{17,25},{25,17},{2,10},{10... | collective-permute-start | bytes 294920 | tf_op jit(solution)/shard_map/ppermute | solution.py:21
  5.7 3.8 %convolution_convert_fusion = bf16[2,3072,128]{2,1,0:T(8,128)(2,1)S(1)} fusion(bf16[2,384,3072]{2,1,0:T(8,128)(2,1)} %param.2, bf16[384,128]{1,0:T(8,128)(2,1)} %refs_0_.3), kind=kOutput, calls=%fused_computation | convolution fusion | flops 604766208 | bytes 6389760 | tf_op jit(solution)/shard_map/ri,prk->pki/dot_general | solution.py:146
  9.5 0.1 constant_dynamic-slice_fusion.7
  9.5 0.1 collective-permute-start
  9.6 0.0 collective-permute-done.3.refs_3_
  9.6 3.9 %collective-permute-done.2.refs_2_ = bf16[384,128]{1,0:T(8,128)(2,1)S(1)} collective-permute-done((bf16[384,128]{1,0:T(8,128)(2,1)}, bf16[384,128]{1,0:T(8,128)(2,1)S(1)}, u32[]{:S(2)}, u32[]{:S(2)}) %collective-permute-start.2) | collective-permute-done | bytes 98336 | tf_op jit(solution)/shard_map/ppermute | solution.py:21
  13.5 0.0 collective-permute-done.1.refs_1_
  13.5 0.0 copy-done
  13.5 0.4 %shard_map.28.refs_4_ = f32[2,128,128]{2,1,0:T(8,128)S(1)} custom-call(bf16[2,4,2,384,128]{4,3,2,1,0:T(8,128)(2,1)S(1)} %bitcast.21, bf16[384,128]{1,0:T(8,128)(2,1)S(1)} %copy-done, bf16[384,128]{1,0:T(8,128)(2,1)S(1)} %collective-permute-done.1.refs_1_, bf16[384,128]{1,0:T(8,128)(2,1)S(1)} %collective-permute-done.2.refs_2_, ...), custom_call_target="tpu_custom_call" | custom-call | flops 99999997952 | bytes 100000000 | tf_op jit(solution)/shard_map/pallas_call | solution.py:42
  14.0 0.0 collective-permute-done.left_ref
  14.0 0.4 %shard_map.29 = f32[2,128,128]{2,1,0:T(8,128)S(1)} custom-call(bf16[2,4,1,384,128]{4,3,2,1,0:T(8,128)(2,1)S(1)} %collective-permute-done.left_ref, bf16[384,128]{1,0:T(8,128)(2,1)S(1)} %copy-done, bf16[384,128]{1,0:T(8,128)(2,1)S(1)} %collective-permute-done.1.refs_1_, bf16[384,128]{1,0:T(8,128)(2,1)S(1)} %collective-permute-done.2.refs_2_, ...), custom_call_target="tpu_custom_call" | custom-call | flops 100663296 | bytes 100663 | tf_op jit(solution)/shard_map/pallas_call | solution.py:42
  14.4 0.1 copy.13
  14.5 0.1 collective-permute-start.4
  14.6 1.2 %collective-permute-done.4 = f32[2,4,16,128]{3,0,2,1:T(2,128)S(1)} collective-permute-done((f32[2,4,16,128]{3,0,2,1:T(2,128)S(1)}, f32[2,4,16,128]{3,0,2,1:T(2,128)S(1)}, u32[]{:S(2)}, u32[]{:S(2)}) %collective-permute-start.4) | collective-permute-done | bytes 65568 | tf_op jit(solution)/shard_map/ppermute | solution.py:156
  15.8 0.1 fusion.1
  15.9 2.6 %collective-permute-start.7 = (bf16[2,4,16,128]{3,0,2,1:T(2,128)(2,1)S(1)}, bf16[2,4,16,128]{3,0,2,1:T(2,128)(2,1)S(1)}, u32[]{:S(2)}, u32[]{:S(2)}) collective-permute-start(bf16[2,4,16,128]{3,0,2,1:T(2,128)(2,1)S(1)} %fusion.1), channel_id=1, source_target_pairs={{0,24},{8,16},{16,8},{24,0},{1,25},{9,17},{17,9},{25,1},{2,26},{10... | collective-permute-start | bytes 98312 | tf_op jit(solution)/shard_map/ppermute | solution.py:21
  18.4 0.0 collective-permute-start.6
  18.4 1.9 %collective-permute-start.5 = (bf16[2,4,16,128]{3,0,2,1:T(2,128)(2,1)S(1)}, bf16[2,4,16,128]{3,0,2,1:T(2,128)(2,1)S(1)}, u32[]{:S(2)}, u32[]{:S(2)}) collective-permute-start(bf16[2,4,16,128]{3,0,2,1:T(2,128)(2,1)S(1)} %fusion.1), channel_id=1, source_target_pairs={{0,8},{8,0},{16,24},{24,16},{1,9},{9,1},{17,25},{25,17},{2,10},{10... | collective-permute-start | bytes 98312 | tf_op jit(solution)/shard_map/ppermute | solution.py:21
  20.3 1.3 %collective-permute-done.7 = bf16[2,4,16,128]{3,0,2,1:T(2,128)(2,1)S(1)} collective-permute-done((bf16[2,4,16,128]{3,0,2,1:T(2,128)(2,1)S(1)}, bf16[2,4,16,128]{3,0,2,1:T(2,128)(2,1)S(1)}, u32[]{:S(2)}, u32[]{:S(2)}) %collective-permute-start.7) | collective-permute-done | bytes 32800 | tf_op jit(solution)/shard_map/ppermute | solution.py:21
  21.6 1.6 %collective-permute-done.6 = bf16[2,4,16,128]{3,0,2,1:T(2,128)(2,1)S(1)} collective-permute-done((bf16[2,4,16,128]{3,0,2,1:T(2,128)(2,1)S(1)}, bf16[2,4,16,128]{3,0,2,1:T(2,128)(2,1)S(1)}, u32[]{:S(2)}, u32[]{:S(2)}) %collective-permute-start.6) | collective-permute-done | bytes 32800 | tf_op jit(solution)/shard_map/ppermute | solution.py:21
  23.2 0.0 collective-permute-done.5
  23.3 0.1 add_convert_fusion
  23.4 0.1 pad_maximum_fusion.2
  23.5 2.5 %collective-permute-start.8 = (bf16[2,2,16,128]{3,0,2,1:T(2,128)(2,1)S(1)}, bf16[2,2,16,128]{3,0,2,1:T(2,128)(2,1)S(1)}, u32[]{:S(2)}, u32[]{:S(2)}) collective-permute-start(bf16[2,2,16,128]{3,0,2,1:T(2,128)(2,1)S(1)} %get-tuple-element.19), channel_id=1, source_target_pairs={{0,3},{1,2},{2,1},{3,0},{4,7},{5,6},{6,5},{7,4},{8,11},{9,10},{10,... | collective-permute-start | bytes 49160 | tf_op jit(solution)/shard_map/ppermute | solution.py:21
  26.0 0.5 %collective-permute-start.9 = (bf16[2,2,16,128]{3,0,2,1:T(2,128)(2,1)S(1)}, bf16[2,2,16,128]{3,0,2,1:T(2,128)(2,1)S(1)}, u32[]{:S(2)}, u32[]{:S(2)}) collective-permute-start(bf16[2,2,16,128]{3,0,2,1:T(2,128)(2,1)S(1)} %get-tuple-element.20), channel_id=1, source_target_pairs={{0,2},{1,3},{2,0},{3,1},{4,6},{5,7},{6,4},{7,5},{8,10},{9,11},{10,... | collective-permute-start | bytes 49160 | tf_op jit(solution)/shard_map/ppermute | solution.py:21
  26.5 0.5 %collective-permute-start.10 = (bf16[2,2,16,128]{3,0,2,1:T(2,128)(2,1)S(1)}, bf16[2,2,16,128]{3,0,2,1:T(2,128)(2,1)S(1)}, u32[]{:S(2)}, u32[]{:S(2)}) collective-permute-start(bf16[2,2,16,128]{3,0,2,1:T(2,128)(2,1)S(1)} %get-tuple-element.21), channel_id=1, source_target_pairs={{0,1},{1,0},{2,3},{3,2},{4,5},{5,4},{6,7},{7,6},{8,9},{9,8},{10,11... | collective-permute-start | bytes 49160 | tf_op jit(solution)/shard_map/ppermute | solution.py:21
  27.0 1.1 %collective-permute-done.8 = bf16[2,2,16,128]{3,0,2,1:T(2,128)(2,1)S(1)} collective-permute-done((bf16[2,2,16,128]{3,0,2,1:T(2,128)(2,1)S(1)}, bf16[2,2,16,128]{3,0,2,1:T(2,128)(2,1)S(1)}, u32[]{:S(2)}, u32[]{:S(2)}) %collective-permute-start.8) | collective-permute-done | bytes 16416 | tf_op jit(solution)/shard_map/ppermute | solution.py:21
  28.2 1.5 %collective-permute-done.9 = bf16[2,2,16,128]{3,0,2,1:T(2,128)(2,1)S(1)} collective-permute-done((bf16[2,2,16,128]{3,0,2,1:T(2,128)(2,1)S(1)}, bf16[2,2,16,128]{3,0,2,1:T(2,128)(2,1)S(1)}, u32[]{:S(2)}, u32[]{:S(2)}) %collective-permute-start.9) | collective-permute-done | bytes 16416 | tf_op jit(solution)/shard_map/ppermute | solution.py:21
  29.7 0.5 %collective-permute-done.10 = bf16[2,2,16,128]{3,0,2,1:T(2,128)(2,1)S(1)} collective-permute-done((bf16[2,2,16,128]{3,0,2,1:T(2,128)(2,1)S(1)}, bf16[2,2,16,128]{3,0,2,1:T(2,128)(2,1)S(1)}, u32[]{:S(2)}, u32[]{:S(2)}) %collective-permute-start.10) | collective-permute-done | bytes 16416 | tf_op jit(solution)/shard_map/ppermute | solution.py:21
  30.2 0.1 pad_maximum_fusion
  30.3 0.1 collective-permute-start.11
  30.4 1.3 %shard_map.30 = (bf16[2048,1024]{1,0:T(8,128)(2,1)S(1)}, bf16[2048,8]{1,0:T(8,128)(2,1)S(1)}) custom-call(bf16[8,2048]{1,0:T(8,128)(2,1)S(1)} %get-tuple-element.13.row_ref, bf16[8,2048]{1,0:T(8,128)(2,1)S(1)} %get-tuple-element.12.col_ref), custom_call_target="tpu_custom_call" | custom-call | flops 33554432 | bytes 4194304 | tf_op jit(solution)/shard_map/pallas_call | solution.py:102
  31.8 0.0 collective-permute-done.11
  31.8 5.9 %shard_map.31 = bf16[2048,4096]{1,0:T(8,128)(2,1)} custom-call(bf16[2048,1024]{1,0:T(8,128)(2,1)S(1)} %get-tuple-element.7.head_ref, bf16[2048,8]{1,0:T(8,128)(2,1)S(1)} %get-tuple-element.8.flipped_ref, bf16[8,3072]{1,0:T(8,128)(2,1)S(1)} %pad_maximum_fusion.1.col_ref), custom_call_target="tpu_custom_call" | custom-call | flops 100663296 | bytes 16777216 | tf_op jit(solution)/shard_map/pallas_call | solution.py:122
  (5 shorter events, 0.1 us)
Async XLA Ops:
  0.0 13.5 %copy-start = (bf16[384,128]{1,0:T(8,128)(2,1)S(1)}, bf16[384,128]{1,0:T(8,128)(2,1)}, u32[]{:S(2)}) copy-start(bf16[384,128]{1,0:T(8,128)(2,1)} %refs_0_.3) | copy-start | bytes 294916
  0.0 9.6 %collective-permute-start.3 = (bf16[384,128]{1,0:T(8,128)(2,1)}, bf16[384,128]{1,0:T(8,128)(2,1)S(1)}, u32[]{:S(2)}, u32[]{:S(2)}) collective-permute-start(bf16[384,128]{1,0:T(8,128)(2,1)} %refs_0_.3), channel_id=1, source_target_pairs={{0,24},{8,16},{16,8},{24,0},{1,25},{9,17},{17,9},{25,1},{2,26},{10... | collective-permute-start | bytes 294920 | tf_op jit(solution)/shard_map/ppermute | solution.py:21
  5.1 8.5 %collective-permute-start.2 = (bf16[384,128]{1,0:T(8,128)(2,1)}, bf16[384,128]{1,0:T(8,128)(2,1)S(1)}, u32[]{:S(2)}, u32[]{:S(2)}) collective-permute-start(bf16[384,128]{1,0:T(8,128)(2,1)} %refs_0_.3), channel_id=1, source_target_pairs={{0,16},{8,24},{16,0},{24,8},{1,17},{9,25},{17,1},{25,9},{2,18},{10... | collective-permute-start | bytes 294920 | tf_op jit(solution)/shard_map/ppermute | solution.py:21
  5.1 8.5 %collective-permute-start.1 = (bf16[384,128]{1,0:T(8,128)(2,1)}, bf16[384,128]{1,0:T(8,128)(2,1)S(1)}, u32[]{:S(2)}, u32[]{:S(2)}) collective-permute-start(bf16[384,128]{1,0:T(8,128)(2,1)} %refs_0_.3), channel_id=1, source_target_pairs={{0,8},{8,0},{16,24},{24,16},{1,9},{9,1},{17,25},{25,17},{2,10},{10... | collective-permute-start | bytes 294920 | tf_op jit(solution)/shard_map/ppermute | solution.py:21
  9.5 4.4 %collective-permute-start = (bf16[2,4,1,384,128]{4,3,2,1,0:T(8,128)(2,1)S(1)}, bf16[2,4,1,384,128]{4,3,2,1,0:T(8,128)(2,1)S(1)}, u32[]{:S(2)}, u32[]{:S(2)}) collective-permute-start(bf16[2,4,1,384,128]{4,3,2,1,0:T(8,128)(2,1)S(1)} %constant_dynamic-slice_fusion.7), channel_id=1, source_target_pairs={{0,4},{4,0},{1,5},{5,1},{2,6},{6,2},{3,7},{7,3},{8,12},{12,8},{9,1... | collective-permute-start | bytes 2359304 | tf_op jit(solution)/shard_map/ppermute | solution.py:149
  14.5 1.3 %collective-permute-start.4 = (f32[2,4,16,128]{3,0,2,1:T(2,128)S(1)}, f32[2,4,16,128]{3,0,2,1:T(2,128)S(1)}, u32[]{:S(2)}, u32[]{:S(2)}) collective-permute-start(f32[2,4,16,128]{3,0,2,1:T(2,128)S(1)} %bitcast.23), channel_id=1, source_target_pairs={{0,4},{4,0},{1,5},{5,1},{2,6},{6,2},{3,7},{7,3},{8,12},{12,8},{9,1... | collective-permute-start | bytes 196616 | tf_op jit(solution)/shard_map/ppermute | solution.py:156
  15.9 5.8 %collective-permute-start.7 = (bf16[2,4,16,128]{3,0,2,1:T(2,128)(2,1)S(1)}, bf16[2,4,16,128]{3,0,2,1:T(2,128)(2,1)S(1)}, u32[]{:S(2)}, u32[]{:S(2)}) collective-permute-start(bf16[2,4,16,128]{3,0,2,1:T(2,128)(2,1)S(1)} %fusion.1), channel_id=1, source_target_pairs={{0,24},{8,16},{16,8},{24,0},{1,25},{9,17},{17,9},{25,1},{2,26},{10... | collective-permute-start | bytes 98312 | tf_op jit(solution)/shard_map/ppermute | solution.py:21
  18.4 4.8 %collective-permute-start.6 = (bf16[2,4,16,128]{3,0,2,1:T(2,128)(2,1)S(1)}, bf16[2,4,16,128]{3,0,2,1:T(2,128)(2,1)S(1)}, u32[]{:S(2)}, u32[]{:S(2)}) collective-permute-start(bf16[2,4,16,128]{3,0,2,1:T(2,128)(2,1)S(1)} %fusion.1), channel_id=1, source_target_pairs={{0,16},{8,24},{16,0},{24,8},{1,17},{9,25},{17,1},{25,9},{2,18},{10... | collective-permute-start | bytes 98312 | tf_op jit(solution)/shard_map/ppermute | solution.py:21
  18.4 4.8 %collective-permute-start.5 = (bf16[2,4,16,128]{3,0,2,1:T(2,128)(2,1)S(1)}, bf16[2,4,16,128]{3,0,2,1:T(2,128)(2,1)S(1)}, u32[]{:S(2)}, u32[]{:S(2)}) collective-permute-start(bf16[2,4,16,128]{3,0,2,1:T(2,128)(2,1)S(1)} %fusion.1), channel_id=1, source_target_pairs={{0,8},{8,0},{16,24},{24,16},{1,9},{9,1},{17,25},{25,17},{2,10},{10... | collective-permute-start | bytes 98312 | tf_op jit(solution)/shard_map/ppermute | solution.py:21
  23.5 4.7 %collective-permute-start.8 = (bf16[2,2,16,128]{3,0,2,1:T(2,128)(2,1)S(1)}, bf16[2,2,16,128]{3,0,2,1:T(2,128)(2,1)S(1)}, u32[]{:S(2)}, u32[]{:S(2)}) collective-permute-start(bf16[2,2,16,128]{3,0,2,1:T(2,128)(2,1)S(1)} %get-tuple-element.19), channel_id=1, source_target_pairs={{0,3},{1,2},{2,1},{3,0},{4,7},{5,6},{6,5},{7,4},{8,11},{9,10},{10,... | collective-permute-start | bytes 49160 | tf_op jit(solution)/shard_map/ppermute | solution.py:21
  26.0 3.7 %collective-permute-start.9 = (bf16[2,2,16,128]{3,0,2,1:T(2,128)(2,1)S(1)}, bf16[2,2,16,128]{3,0,2,1:T(2,128)(2,1)S(1)}, u32[]{:S(2)}, u32[]{:S(2)}) collective-permute-start(bf16[2,2,16,128]{3,0,2,1:T(2,128)(2,1)S(1)} %get-tuple-element.20), channel_id=1, source_target_pairs={{0,2},{1,3},{2,0},{3,1},{4,6},{5,7},{6,4},{7,5},{8,10},{9,11},{10,... | collective-permute-start | bytes 49160 | tf_op jit(solution)/shard_map/ppermute | solution.py:21
  26.5 3.7 %collective-permute-start.10 = (bf16[2,2,16,128]{3,0,2,1:T(2,128)(2,1)S(1)}, bf16[2,2,16,128]{3,0,2,1:T(2,128)(2,1)S(1)}, u32[]{:S(2)}, u32[]{:S(2)}) collective-permute-start(bf16[2,2,16,128]{3,0,2,1:T(2,128)(2,1)S(1)} %get-tuple-element.21), channel_id=1, source_target_pairs={{0,1},{1,0},{2,3},{3,2},{4,5},{5,4},{6,7},{7,6},{8,9},{9,8},{10,11... | collective-permute-start | bytes 49160 | tf_op jit(solution)/shard_map/ppermute | solution.py:21
  30.3 1.4 %collective-permute-start.11 = (bf16[8,1,16,128]{3,0,2,1:T(8,128)(2,1)S(1)}, bf16[8,1,16,128]{3,0,2,1:T(8,128)(2,1)S(1)}, u32[]{:S(2)}, u32[]{:S(2)}) collective-permute-start(bf16[8,1,16,128]{3,0,2,1:T(8,128)(2,1)S(1)} %get-tuple-element.11), channel_id=1, source_target_pairs={{0,4},{4,0},{1,5},{5,1},{2,6},{6,2},{3,7},{7,3},{8,12},{12,8},{9,1... | collective-permute-start | bytes 98312 | tf_op jit(solution)/shard_map/ppermute | solution.py:173

commit v2 on v1

--- a/solution.py
+++ b/solution.py
@@ -51,88 +51,106 @@
     )(left, *held, *before)
 
 
-def head_kernel(slab, row_ref, col_ref, head_ref, flipped_ref):
+BLOCKS = 4
+
+
+def block_product(flipped_ref, col_ref, into_ref, n, size):
+    at = pl.ds(pl.multiple_of(n * size, size), size)
+    return at, jnp.dot(
+        flipped_ref[at, :], col_ref[...], preferred_element_type=jnp.float32
+    ).astype(into_ref.dtype)
+
+
+def head_kernel(size, row_ref, col_ref, head_ref, flipped_ref):
     flipped_ref[...] = row_ref[...].astype(jnp.float32).T.astype(flipped_ref.dtype)
-    for n in range(head_ref.shape[1] // slab):
-        at = pl.ds(n * slab, slab)
-        head_ref[:, at] = jnp.dot(
-            flipped_ref[...], col_ref[:, at], preferred_element_type=jnp.float32
-        ).astype(head_ref.dtype)
-
-
-def rest_kernel(slab, side, head_ref, flipped_ref, col_ref, out_ref, block, sems):
-    heads = head_ref.shape[1] // slab
-    own, per = sems.shape[0] // CORES, side // slab
+    for n in range(head_ref.shape[0] // size):
+        at, made = block_product(flipped_ref, col_ref, head_ref, n, size)
+        head_ref[at, :] = made
+
+
+def rest_kernel(side, size, head_ref, flipped_ref, own_ref, got_ref, out_ref, own, other, sems):
     core = lax.axis_index("core")
-
-    def write(source, n, t):
-        s, owner = t % own, (core + t // own) % CORES
-        to = (s // per * CORES + owner) * side + s % per * slab
-        return pltpu.make_async_copy(
-            source.at[:, pl.ds(pl.multiple_of(n * slab, slab), slab)],
-            out_ref.at[:, pl.ds(pl.multiple_of(to, slab), slab)],
-            sems.at[t],
-        )
-
-    for n in range(heads):
-        write(head_ref, n, n).start()
-
-    rest = sems.shape[0] - heads
-
-    @pl.loop(0, rest, unroll=3 if rest % 3 == 0 else 1)
-    def _(n):
-        at = pl.ds(pl.multiple_of(n * slab, slab), slab)
-        block[:, at] = jnp.dot(
-            flipped_ref[...], col_ref[:, at], preferred_element_type=jnp.float32
-        ).astype(block.dtype)
-        write(block, n, n + heads).start()
-
-    for n in range(heads):
-        write(head_ref, n, n).wait()
-
-    @pl.loop(0, rest)
-    def _(n):
-        write(block, n, n + heads).wait()
-
-
-def head_product(row_part, col_part, slab):
+    parts = own_ref.shape[1] // side
+    heads = head_ref.shape[0] // size
+
+    def writes(source, n, to, owner):
+        for part in range(parts):
+            yield pltpu.make_async_copy(
+                source.at[pl.ds(pl.multiple_of(n * size, size), size), pl.ds(part * side, side)],
+                out_ref.at[
+                    pl.ds(pl.multiple_of(to * size, size), size),
+                    pl.ds(pl.multiple_of((part * CORES + owner) * side, side), side),
+                ],
+                sems.at[owner, to, part],
+            )
+
+    def each(act):
+        for n in range(heads):
+            for copy in writes(head_ref, n, n, core):
+                act(copy)
+
+        @pl.loop(0, BLOCKS - heads, unroll=act is start)
+        def _(n):
+            if act is start:
+                to = n + heads
+                made = block_product(flipped_ref, own_ref, own, to, size)[1]
+                own[pl.ds(pl.multiple_of(n * size, size), size), :] = made
+            for copy in writes(own, n, n + heads, core):
+                act(copy)
+
+        @pl.loop(0, BLOCKS, unroll=act is start)
+        def _(n):
+            if act is start:
+                at, made = block_product(flipped_ref, got_ref, other, n, size)
+                other[at, :] = made
+            for copy in writes(other, n, n, 1 - core):
+                act(copy)
+
+    def start(copy):
+        copy.start()
+
+    each(start)
+    each(lambda copy: copy.wait())
+
+
+def head_product(row_part, col_part):
     vecs, rows = row_part.shape
-    width = slab * max(1, col_part.shape[1] // slab // 2)
+    width = col_part.shape[1]
     whole = pl.BlockSpec(memory_space=pltpu.VMEM)
     return pl.pallas_call(
-        functools.partial(head_kernel, slab),
+        functools.partial(head_kernel, rows // BLOCKS),
         out_shape=(
-            jax.ShapeDtypeStruct((rows, width), jnp.bfloat16),
+            jax.ShapeDtypeStruct((rows // 2, width), jnp.bfloat16),
             jax.ShapeDtypeStruct((rows, vecs), jnp.bfloat16),
         ),
         in_specs=[whole] * 2,
         out_specs=(whole, whole),
         compiler_params=pltpu.CompilerParams(vmem_limit_bytes=24 << 20),
         cost_estimate=pl.CostEstimate(
-            flops=2 * vecs * rows * width, bytes_accessed=2 * rows * width, transcendentals=0
+            flops=vecs * rows * width, bytes_accessed=rows * width, transcendentals=0
         ),
     )(row_part, col_part)
 
 
-def rest_product(head, flipped, col_rest, side, slab):
+def rest_product(head, flipped, col_own, col_got, side):
     rows, vecs = flipped.shape
-    width = col_rest.shape[1]
-    cols = head.shape[1] + width
+    width = col_own.shape[1]
     whole = pl.BlockSpec(memory_space=pltpu.VMEM)
     return pl.pallas_call(
-        functools.partial(rest_kernel, slab, side),
-        out_shape=jax.ShapeDtypeStruct((rows, cols), jnp.bfloat16),
-        in_specs=[whole] * 3,
+        functools.partial(rest_kernel, side, rows // BLOCKS),
+        out_shape=jax.ShapeDtypeStruct((rows, 2 * width), jnp.bfloat16),
+        in_specs=[whole] * 4,
         out_specs=pl.BlockSpec(memory_space=pl.ANY),
         scratch_shapes=[
+            pltpu.VMEM((rows - head.shape[0], width), jnp.bfloat16),
             pltpu.VMEM((rows, width), jnp.bfloat16),
-            pltpu.SemaphoreType.DMA((cols // slab,)),
+            pltpu.SemaphoreType.DMA((CORES, BLOCKS, width // side)),
         ],
         compiler_params=pltpu.CompilerParams(vmem_limit_bytes=32 << 20),
         cost_estimate=pl.CostEstimate(
-            flops=2 * vecs * rows * width, bytes_accessed=2 * rows * cols, transcendentals=0
-        ),
-    )(head, flipped, col_rest)
+            flops=3 * vecs * rows * width, bytes_accessed=4 * rows * width, transcendentals=0
+        ),
+    )(head, flipped, col_own, col_got)
 
 
 def body(cholesky, coeffs):
@@ -171,11 +189,8 @@
     row_part, col_own = seen[:, :1].reshape(vecs, -1), seen[:, 1:].reshape(vecs, -1)
 
     col_got = lax.ppermute(seen[:, 1:], "core", SWAP).reshape(vecs, -1)
-    side = span * orbitals
-    slab = min(side, 512)
-    head, flipped = head_product(row_part, col_own, slab)
-    col_rest = jnp.concatenate([col_own[:, head.shape[1] :], col_got], 1)
-    return rest_product(head, flipped, col_rest, side, slab)
+    head, flipped = head_product(row_part, col_own)
+    return rest_product(head, flipped, col_own, col_got, span * orbitals)
 
 
 def solution(mesh):

time: 37.9 us -> 37.9 us (level)
  no operation moved by 1% of the time
where the time goes in v2:
time: 37.9 us; the launch traced here: 37.7 us
  starting transfers between devices  13.9 us (37%)
  waiting for transfers between devices  11.3 us (30%)
  Pallas kernels  8.07 us (21%)
  matrix products  3.77 us (10%)
    ppermute x9, starting transfers between devices, flip(): return lax.ppermute(array, axis, [(d, d ^ step) for d in range(count)])  13.7 us
    ppermute x9, waiting for transfers between devices, flip(): return lax.ppermute(array, axis, [(d, d ^ step) for d in range(count)])  10.1 us
    pallas_call x1, Pallas kernels, rest_product(): pl.pallas_call(functools.partial(rest_kernel, side, rows // BLOCKS), out_...  5.93 us
    dot_general x1, matrix products, body(): jnp.einsum('ri,prk->pki', coeffs, cholesky, preferred_element_type=jnp.fl...  3.77 us
    pallas_call x1, Pallas kernels, head_product(): pl.pallas_call(functools.partial(head_kernel, rows // BLOCKS), out_shape=...  1.31 us
    ppermute x1, waiting for transfers between devices, body(): lax.ppermute(lax.dynamic_index_in_dim(partial, 1 - core, 2, keepdims=Fals...  1.24 us
    pallas_call x2, Pallas kernels, project(): pl.pallas_call(functools.partial(project_kernel, nz), out_shape=jax.Shape...  0.83 us
  transfers between devices with their start and end apart: 12, of which 7 were waited for; matrix products, arithmetic and copies ran while one was open for 10% of the time, Pallas kernels for 5%

profile of v2, /device:TPU:0, one launch (start us, length us, event | category | flops | bytes accessed | tf_op | source)
XLA Modules:
  0.0 37.7 jit_solution(11184662502238964864)
XLA Ops:
  0.0 0.0 copy-start
  0.0 5.0 %collective-permute-start.3 = (bf16[384,128]{1,0:T(8,128)(2,1)}, bf16[384,128]{1,0:T(8,128)(2,1)S(1)}, u32[]{:S(2)}, u32[]{:S(2)}) collective-permute-start(bf16[384,128]{1,0:T(8,128)(2,1)} %refs_0_.3), channel_id=1, source_target_pairs={{0,24},{8,16},{16,8},{24,0},{1,25},{9,17},{17,9},{25,1},{2,26},{10... | collective-permute-start | bytes 294920 | tf_op jit(solution)/shard_map/ppermute | solution.py:21
  5.1 0.0 collective-permute-start.2
  5.1 0.6 %collective-permute-start.1 = (bf16[384,128]{1,0:T(8,128)(2,1)}, bf16[384,128]{1,0:T(8,128)(2,1)S(1)}, u32[]{:S(2)}, u32[]{:S(2)}) collective-permute-start(bf16[384,128]{1,0:T(8,128)(2,1)} %refs_0_.3), channel_id=1, source_target_pairs={{0,8},{8,0},{16,24},{24,16},{1,9},{9,1},{17,25},{25,17},{2,10},{10... | collective-permute-start | bytes 294920 | tf_op jit(solution)/shard_map/ppermute | solution.py:21
  5.7 3.8 %convolution_convert_fusion = bf16[2,3072,128]{2,1,0:T(8,128)(2,1)S(1)} fusion(bf16[2,384,3072]{2,1,0:T(8,128)(2,1)} %param.2, bf16[384,128]{1,0:T(8,128)(2,1)} %refs_0_.3), kind=kOutput, calls=%fused_computation | convolution fusion | flops 604766208 | bytes 6389760 | tf_op jit(solution)/shard_map/ri,prk->pki/dot_general | solution.py:164
  9.5 0.1 constant_dynamic-slice_fusion.7
  9.5 0.1 collective-permute-start
  9.6 0.0 collective-permute-done.3.refs_3_
  9.6 3.9 %collective-permute-done.2.refs_2_ = bf16[384,128]{1,0:T(8,128)(2,1)S(1)} collective-permute-done((bf16[384,128]{1,0:T(8,128)(2,1)}, bf16[384,128]{1,0:T(8,128)(2,1)S(1)}, u32[]{:S(2)}, u32[]{:S(2)}) %collective-permute-start.2) | collective-permute-done | bytes 98336 | tf_op jit(solution)/shard_map/ppermute | solution.py:21
  13.5 0.0 collective-permute-done.1.refs_1_
  13.5 0.0 copy-done
  13.5 0.4 %shard_map.28.refs_4_ = f32[2,128,128]{2,1,0:T(8,128)S(1)} custom-call(bf16[2,4,2,384,128]{4,3,2,1,0:T(8,128)(2,1)S(1)} %bitcast.21, bf16[384,128]{1,0:T(8,128)(2,1)S(1)} %copy-done, bf16[384,128]{1,0:T(8,128)(2,1)S(1)} %collective-permute-done.1.refs_1_, bf16[384,128]{1,0:T(8,128)(2,1)S(1)} %collective-permute-done.2.refs_2_, ...), custom_call_target="tpu_custom_call" | custom-call | flops 99999997952 | bytes 100000000 | tf_op jit(solution)/shard_map/pallas_call | solution.py:42
  14.0 0.0 collective-permute-done.left_ref
  14.0 0.4 %shard_map.29 = f32[2,128,128]{2,1,0:T(8,128)S(1)} custom-call(bf16[2,4,1,384,128]{4,3,2,1,0:T(8,128)(2,1)S(1)} %collective-permute-done.left_ref, bf16[384,128]{1,0:T(8,128)(2,1)S(1)} %copy-done, bf16[384,128]{1,0:T(8,128)(2,1)S(1)} %collective-permute-done.1.refs_1_, bf16[384,128]{1,0:T(8,128)(2,1)S(1)} %collective-permute-done.2.refs_2_, ...), custom_call_target="tpu_custom_call" | custom-call | flops 100663296 | bytes 100663 | tf_op jit(solution)/shard_map/pallas_call | solution.py:42
  14.4 0.1 copy.13
  14.5 0.1 collective-permute-start.4
  14.6 1.2 %collective-permute-done.4 = f32[2,4,16,128]{3,0,2,1:T(2,128)S(1)} collective-permute-done((f32[2,4,16,128]{3,0,2,1:T(2,128)S(1)}, f32[2,4,16,128]{3,0,2,1:T(2,128)S(1)}, u32[]{:S(2)}, u32[]{:S(2)}) %collective-permute-start.4) | collective-permute-done | bytes 65568 | tf_op jit(solution)/shard_map/ppermute | solution.py:174
  15.8 0.1 fusion.1
  15.9 2.6 %collective-permute-start.7 = (bf16[2,4,16,128]{3,0,2,1:T(2,128)(2,1)S(1)}, bf16[2,4,16,128]{3,0,2,1:T(2,128)(2,1)S(1)}, u32[]{:S(2)}, u32[]{:S(2)}) collective-permute-start(bf16[2,4,16,128]{3,0,2,1:T(2,128)(2,1)S(1)} %fusion.1), channel_id=1, source_target_pairs={{0,24},{8,16},{16,8},{24,0},{1,25},{9,17},{17,9},{25,1},{2,26},{10... | collective-permute-start | bytes 98312 | tf_op jit(solution)/shard_map/ppermute | solution.py:21
  18.4 0.0 collective-permute-start.6
  18.4 1.9 %collective-permute-start.5 = (bf16[2,4,16,128]{3,0,2,1:T(2,128)(2,1)S(1)}, bf16[2,4,16,128]{3,0,2,1:T(2,128)(2,1)S(1)}, u32[]{:S(2)}, u32[]{:S(2)}) collective-permute-start(bf16[2,4,16,128]{3,0,2,1:T(2,128)(2,1)S(1)} %fusion.1), channel_id=1, source_target_pairs={{0,8},{8,0},{16,24},{24,16},{1,9},{9,1},{17,25},{25,17},{2,10},{10... | collective-permute-start | bytes 98312 | tf_op jit(solution)/shard_map/ppermute | solution.py:21
  20.3 1.3 %collective-permute-done.7 = bf16[2,4,16,128]{3,0,2,1:T(2,128)(2,1)S(1)} collective-permute-done((bf16[2,4,16,128]{3,0,2,1:T(2,128)(2,1)S(1)}, bf16[2,4,16,128]{3,0,2,1:T(2,128)(2,1)S(1)}, u32[]{:S(2)}, u32[]{:S(2)}) %collective-permute-start.7) | collective-permute-done | bytes 32800 | tf_op jit(solution)/shard_map/ppermute | solution.py:21
  21.6 1.6 %collective-permute-done.6 = bf16[2,4,16,128]{3,0,2,1:T(2,128)(2,1)S(1)} collective-permute-done((bf16[2,4,16,128]{3,0,2,1:T(2,128)(2,1)S(1)}, bf16[2,4,16,128]{3,0,2,1:T(2,128)(2,1)S(1)}, u32[]{:S(2)}, u32[]{:S(2)}) %collective-permute-start.6) | collective-permute-done | bytes 32800 | tf_op jit(solution)/shard_map/ppermute | solution.py:21
  23.2 0.0 collective-permute-done.5
  23.3 0.1 add_convert_fusion
  23.4 0.1 pad_maximum_fusion.1
  23.5 2.5 %collective-permute-start.8 = (bf16[2,2,16,128]{3,0,2,1:T(2,128)(2,1)S(1)}, bf16[2,2,16,128]{3,0,2,1:T(2,128)(2,1)S(1)}, u32[]{:S(2)}, u32[]{:S(2)}) collective-permute-start(bf16[2,2,16,128]{3,0,2,1:T(2,128)(2,1)S(1)} %get-tuple-element.19), channel_id=1, source_target_pairs={{0,3},{1,2},{2,1},{3,0},{4,7},{5,6},{6,5},{7,4},{8,11},{9,10},{10,... | collective-permute-start | bytes 49160 | tf_op jit(solution)/shard_map/ppermute | solution.py:21
  26.0 0.5 %collective-permute-start.9 = (bf16[2,2,16,128]{3,0,2,1:T(2,128)(2,1)S(1)}, bf16[2,2,16,128]{3,0,2,1:T(2,128)(2,1)S(1)}, u32[]{:S(2)}, u32[]{:S(2)}) collective-permute-start(bf16[2,2,16,128]{3,0,2,1:T(2,128)(2,1)S(1)} %get-tuple-element.20), channel_id=1, source_target_pairs={{0,2},{1,3},{2,0},{3,1},{4,6},{5,7},{6,4},{7,5},{8,10},{9,11},{10,... | collective-permute-start | bytes 49160 | tf_op jit(solution)/shard_map/ppermute | solution.py:21
  26.5 0.5 %collective-permute-start.10 = (bf16[2,2,16,128]{3,0,2,1:T(2,128)(2,1)S(1)}, bf16[2,2,16,128]{3,0,2,1:T(2,128)(2,1)S(1)}, u32[]{:S(2)}, u32[]{:S(2)}) collective-permute-start(bf16[2,2,16,128]{3,0,2,1:T(2,128)(2,1)S(1)} %get-tuple-element.21), channel_id=1, source_target_pairs={{0,1},{1,0},{2,3},{3,2},{4,5},{5,4},{6,7},{7,6},{8,9},{9,8},{10,11... | collective-permute-start | bytes 49160 | tf_op jit(solution)/shard_map/ppermute | solution.py:21
  27.0 1.1 %collective-permute-done.8 = bf16[2,2,16,128]{3,0,2,1:T(2,128)(2,1)S(1)} collective-permute-done((bf16[2,2,16,128]{3,0,2,1:T(2,128)(2,1)S(1)}, bf16[2,2,16,128]{3,0,2,1:T(2,128)(2,1)S(1)}, u32[]{:S(2)}, u32[]{:S(2)}) %collective-permute-start.8) | collective-permute-done | bytes 16416 | tf_op jit(solution)/shard_map/ppermute | solution.py:21
  28.2 1.5 %collective-permute-done.9 = bf16[2,2,16,128]{3,0,2,1:T(2,128)(2,1)S(1)} collective-permute-done((bf16[2,2,16,128]{3,0,2,1:T(2,128)(2,1)S(1)}, bf16[2,2,16,128]{3,0,2,1:T(2,128)(2,1)S(1)}, u32[]{:S(2)}, u32[]{:S(2)}) %collective-permute-start.9) | collective-permute-done | bytes 16416 | tf_op jit(solution)/shard_map/ppermute | solution.py:21
  29.7 0.5 %collective-permute-done.10 = bf16[2,2,16,128]{3,0,2,1:T(2,128)(2,1)S(1)} collective-permute-done((bf16[2,2,16,128]{3,0,2,1:T(2,128)(2,1)S(1)}, bf16[2,2,16,128]{3,0,2,1:T(2,128)(2,1)S(1)}, u32[]{:S(2)}, u32[]{:S(2)}) %collective-permute-start.10) | collective-permute-done | bytes 16416 | tf_op jit(solution)/shard_map/ppermute | solution.py:21
  30.2 0.1 pad_maximum_fusion
  30.3 0.1 collective-permute-start.11
  30.4 1.3 %shard_map.30 = (bf16[1024,2048]{1,0:T(8,128)(2,1)S(1)}, bf16[2048,8]{1,0:T(8,128)(2,1)S(1)}) custom-call(bf16[8,2048]{1,0:T(8,128)(2,1)S(1)} %get-tuple-element.13.row_ref, bf16[8,2048]{1,0:T(8,128)(2,1)S(1)} %get-tuple-element.12.col_ref.own_ref), custom_call_target="tpu_custom_call" | custom-call | flops 33554432 | bytes 4194304 | tf_op jit(solution)/shard_map/pallas_call | solution.py:120
  31.7 0.0 collective-permute-done.11
  31.8 5.9 %shard_map.31 = bf16[2048,4096]{1,0:T(8,128)(2,1)} custom-call(bf16[1024,2048]{1,0:T(8,128)(2,1)S(1)} %get-tuple-element.7.head_ref, bf16[2048,8]{1,0:T(8,128)(2,1)S(1)} %get-tuple-element.8.flipped_ref, bf16[8,2048]{1,0:T(8,128)(2,1)S(1)} %get-tuple-element.12.col_ref.own_ref, bf16[8,2048]{1,0:T(8,128)(2,1)S(1)} %bitcast.23), custom_call_target="tpu_custom_call" | custom-call | flops 100663296 | bytes 16777216 | tf_op jit(solution)/shard_map/pallas_call | solution.py:139
  (3 shorter events, 0.1 us)
Async XLA Ops:
  0.0 13.5 %copy-start = (bf16[384,128]{1,0:T(8,128)(2,1)S(1)}, bf16[384,128]{1,0:T(8,128)(2,1)}, u32[]{:S(2)}) copy-start(bf16[384,128]{1,0:T(8,128)(2,1)} %refs_0_.3) | copy-start | bytes 294916
  0.0 9.6 %collective-permute-start.3 = (bf16[384,128]{1,0:T(8,128)(2,1)}, bf16[384,128]{1,0:T(8,128)(2,1)S(1)}, u32[]{:S(2)}, u32[]{:S(2)}) collective-permute-start(bf16[384,128]{1,0:T(8,128)(2,1)} %refs_0_.3), channel_id=1, source_target_pairs={{0,24},{8,16},{16,8},{24,0},{1,25},{9,17},{17,9},{25,1},{2,26},{10... | collective-permute-start | bytes 294920 | tf_op jit(solution)/shard_map/ppermute | solution.py:21
  5.1 8.5 %collective-permute-start.2 = (bf16[384,128]{1,0:T(8,128)(2,1)}, bf16[384,128]{1,0:T(8,128)(2,1)S(1)}, u32[]{:S(2)}, u32[]{:S(2)}) collective-permute-start(bf16[384,128]{1,0:T(8,128)(2,1)} %refs_0_.3), channel_id=1, source_target_pairs={{0,16},{8,24},{16,0},{24,8},{1,17},{9,25},{17,1},{25,9},{2,18},{10... | collective-permute-start | bytes 294920 | tf_op jit(solution)/shard_map/ppermute | solution.py:21
  5.1 8.5 %collective-permute-start.1 = (bf16[384,128]{1,0:T(8,128)(2,1)}, bf16[384,128]{1,0:T(8,128)(2,1)S(1)}, u32[]{:S(2)}, u32[]{:S(2)}) collective-permute-start(bf16[384,128]{1,0:T(8,128)(2,1)} %refs_0_.3), channel_id=1, source_target_pairs={{0,8},{8,0},{16,24},{24,16},{1,9},{9,1},{17,25},{25,17},{2,10},{10... | collective-permute-start | bytes 294920 | tf_op jit(solution)/shard_map/ppermute | solution.py:21
  9.5 4.4 %collective-permute-start = (bf16[2,4,1,384,128]{4,3,2,1,0:T(8,128)(2,1)S(1)}, bf16[2,4,1,384,128]{4,3,2,1,0:T(8,128)(2,1)S(1)}, u32[]{:S(2)}, u32[]{:S(2)}) collective-permute-start(bf16[2,4,1,384,128]{4,3,2,1,0:T(8,128)(2,1)S(1)} %constant_dynamic-slice_fusion.7), channel_id=1, source_target_pairs={{0,4},{4,0},{1,5},{5,1},{2,6},{6,2},{3,7},{7,3},{8,12},{12,8},{9,1... | collective-permute-start | bytes 2359304 | tf_op jit(solution)/shard_map/ppermute | solution.py:167
  14.5 1.3 %collective-permute-start.4 = (f32[2,4,16,128]{3,0,2,1:T(2,128)S(1)}, f32[2,4,16,128]{3,0,2,1:T(2,128)S(1)}, u32[]{:S(2)}, u32[]{:S(2)}) collective-permute-start(f32[2,4,16,128]{3,0,2,1:T(2,128)S(1)} %bitcast.24), channel_id=1, source_target_pairs={{0,4},{4,0},{1,5},{5,1},{2,6},{6,2},{3,7},{7,3},{8,12},{12,8},{9,1... | collective-permute-start | bytes 196616 | tf_op jit(solution)/shard_map/ppermute | solution.py:174
  15.9 5.8 %collective-permute-start.7 = (bf16[2,4,16,128]{3,0,2,1:T(2,128)(2,1)S(1)}, bf16[2,4,16,128]{3,0,2,1:T(2,128)(2,1)S(1)}, u32[]{:S(2)}, u32[]{:S(2)}) collective-permute-start(bf16[2,4,16,128]{3,0,2,1:T(2,128)(2,1)S(1)} %fusion.1), channel_id=1, source_target_pairs={{0,24},{8,16},{16,8},{24,0},{1,25},{9,17},{17,9},{25,1},{2,26},{10... | collective-permute-start | bytes 98312 | tf_op jit(solution)/shard_map/ppermute | solution.py:21
  18.4 4.8 %collective-permute-start.6 = (bf16[2,4,16,128]{3,0,2,1:T(2,128)(2,1)S(1)}, bf16[2,4,16,128]{3,0,2,1:T(2,128)(2,1)S(1)}, u32[]{:S(2)}, u32[]{:S(2)}) collective-permute-start(bf16[2,4,16,128]{3,0,2,1:T(2,128)(2,1)S(1)} %fusion.1), channel_id=1, source_target_pairs={{0,16},{8,24},{16,0},{24,8},{1,17},{9,25},{17,1},{25,9},{2,18},{10... | collective-permute-start | bytes 98312 | tf_op jit(solution)/shard_map/ppermute | solution.py:21
  18.4 4.8 %collective-permute-start.5 = (bf16[2,4,16,128]{3,0,2,1:T(2,128)(2,1)S(1)}, bf16[2,4,16,128]{3,0,2,1:T(2,128)(2,1)S(1)}, u32[]{:S(2)}, u32[]{:S(2)}) collective-permute-start(bf16[2,4,16,128]{3,0,2,1:T(2,128)(2,1)S(1)} %fusion.1), channel_id=1, source_target_pairs={{0,8},{8,0},{16,24},{24,16},{1,9},{9,1},{17,25},{25,17},{2,10},{10... | collective-permute-start | bytes 98312 | tf_op jit(solution)/shard_map/ppermute | solution.py:21
  23.5 4.7 %collective-permute-start.8 = (bf16[2,2,16,128]{3,0,2,1:T(2,128)(2,1)S(1)}, bf16[2,2,16,128]{3,0,2,1:T(2,128)(2,1)S(1)}, u32[]{:S(2)}, u32[]{:S(2)}) collective-permute-start(bf16[2,2,16,128]{3,0,2,1:T(2,128)(2,1)S(1)} %get-tuple-element.19), channel_id=1, source_target_pairs={{0,3},{1,2},{2,1},{3,0},{4,7},{5,6},{6,5},{7,4},{8,11},{9,10},{10,... | collective-permute-start | bytes 49160 | tf_op jit(solution)/shard_map/ppermute | solution.py:21
  26.0 3.7 %collective-permute-start.9 = (bf16[2,2,16,128]{3,0,2,1:T(2,128)(2,1)S(1)}, bf16[2,2,16,128]{3,0,2,1:T(2,128)(2,1)S(1)}, u32[]{:S(2)}, u32[]{:S(2)}) collective-permute-start(bf16[2,2,16,128]{3,0,2,1:T(2,128)(2,1)S(1)} %get-tuple-element.20), channel_id=1, source_target_pairs={{0,2},{1,3},{2,0},{3,1},{4,6},{5,7},{6,4},{7,5},{8,10},{9,11},{10,... | collective-permute-start | bytes 49160 | tf_op jit(solution)/shard_map/ppermute | solution.py:21
  26.5 3.7 %collective-permute-start.10 = (bf16[2,2,16,128]{3,0,2,1:T(2,128)(2,1)S(1)}, bf16[2,2,16,128]{3,0,2,1:T(2,128)(2,1)S(1)}, u32[]{:S(2)}, u32[]{:S(2)}) collective-permute-start(bf16[2,2,16,128]{3,0,2,1:T(2,128)(2,1)S(1)} %get-tuple-element.21), channel_id=1, source_target_pairs={{0,1},{1,0},{2,3},{3,2},{4,5},{5,4},{6,7},{7,6},{8,9},{9,8},{10,11... | collective-permute-start | bytes 49160 | tf_op jit(solution)/shard_map/ppermute | solution.py:21
  30.3 1.4 %collective-permute-start.11 = (bf16[8,1,16,128]{3,0,2,1:T(8,128)(2,1)S(1)}, bf16[8,1,16,128]{3,0,2,1:T(8,128)(2,1)S(1)}, u32[]{:S(2)}, u32[]{:S(2)}) collective-permute-start(bf16[8,1,16,128]{3,0,2,1:T(8,128)(2,1)S(1)} %get-tuple-element.11), channel_id=1, source_target_pairs={{0,4},{4,0},{1,5},{5,1},{2,6},{6,2},{3,7},{7,3},{8,12},{12,8},{9,1... | collective-permute-start | bytes 98312 | tf_op jit(solution)/shard_map/ppermute | solution.py:191

commit v3 on v2

--- a/solution.py
+++ b/solution.py
@@ -4,16 +4,22 @@
 import jax.numpy as jnp
 from jax import lax
 from jax.experimental import pallas as pl
+from jax.experimental.layout import Layout, with_layout_constraint
 from jax.experimental.pallas import tpu as pltpu
 from jax.sharding import Mesh, PartitionSpec as P
 
 CORES = 2
+LAST = 2
 AO = ("z", "core")
 SWAP = [(0, 1), (1, 0)]
 
 
 def pick(array, index, size, dim):
     return lax.dynamic_slice_in_dim(array, index * size, size, dim)
+
+
+def row_major(array):
+    return with_layout_constraint(array, Layout(tuple(range(array.ndim))))
 
 
 def flip(array, axis, step):
@@ -21,34 +27,37 @@
     return lax.ppermute(array, axis, [(d, d ^ step) for d in range(count)])
 
 
-def project_kernel(nz, left_ref, *refs):
-    held, out_ref = refs[:nz], refs[-1]
+def project_kernel(parts, steps, *refs):
+    lefts, held = refs[:parts], refs[parts : parts + len(steps)]
+    before, out_ref = refs[parts + len(steps) : -1], refs[-1]
     z, core = lax.axis_index("z"), lax.axis_index("core")
     for p in range(out_ref.shape[0]):
-        total = refs[nz][p] if len(refs) > nz + 1 else 0.0
-        for s in range(nz):
-            total += lax.dot_general(
-                left_ref[p, z ^ s, core if left_ref.shape[2] > 1 else 0],
-                held[s][...],
-                (((0,), (0,)), ((), ())),
-                preferred_element_type=jnp.float32,
-            )
+        total = before[0][p] if before else 0.0
+        for left_ref in lefts:
+            for s, block_ref in zip(steps, held):
+                total += lax.dot_general(
+                    left_ref[p, z ^ s, core if left_ref.shape[2] > 1 else 0],
+                    block_ref[...],
+                    (((0,), (0,)), ((), ())),
+                    preferred_element_type=jnp.float32,
+                )
         out_ref[p] = total
 
 
-def project(left, held, *before, flops):
-    vec_dev, nz, _, rows, orbitals = left.shape
+def project(lefts, held, steps, *before, flops=None):
+    vec_dev, nz, _, rows, orbitals = lefts[0].shape
+    work = 2 * len(lefts) * len(steps) * vec_dev * rows * orbitals**2
     whole = pl.BlockSpec(memory_space=pltpu.VMEM)
     return pl.pallas_call(
-        functools.partial(project_kernel, nz),
+        functools.partial(project_kernel, len(lefts), steps),
         out_shape=jax.ShapeDtypeStruct((vec_dev, orbitals, orbitals), jnp.float32),
-        in_specs=[whole] * (1 + nz + len(before)),
+        in_specs=[whole] * (len(lefts) + len(steps) + len(before)),
         out_specs=whole,
         compiler_params=pltpu.CompilerParams(vmem_limit_bytes=32 << 20),
         cost_estimate=pl.CostEstimate(
-            flops=flops, bytes_accessed=flops // 1000, transcendentals=0
-        ),
-    )(left, *held, *before)
+            flops=flops or work, bytes_accessed=(flops or work) // 1000, transcendentals=0
+        ),
+    )(*lefts, *[held[s] for s in steps], *before)
 
 
 BLOCKS = 4
@@ -165,8 +174,11 @@
     left = left.astype(jnp.bfloat16).reshape(vec_dev, nz, CORES, rows, orbitals)
     give = lax.dynamic_slice_in_dim(left, 1 - core, 1, 2)
     got = lax.ppermute(give, "core", SWAP)
-    partial = project(left, held, flops=10**11)
-    partial = project(got, held, partial, flops=2 * got.size * orbitals)
+    late = LAST % nz
+    steps = [s for s in range(nz) if s != late]
+    partial = project([left], held, steps, flops=10**11)
+    partial = project([got], held, steps, partial)
+    partial = project([left, got], held, [late], partial)
 
     span = orbitals // (nz * CORES)
     partial = partial.reshape(vec_dev, nz, CORES, span, orbitals)
@@ -184,7 +196,7 @@
     seen = [jnp.concatenate([row_out, pick(values, chol, wide, 1)], 1)]
     for s in range(n_chol - 1, 0, -1):
         seen.append(flip(jnp.concatenate([row_out, pick(values, chol ^ s, wide, 1)], 1), "chol", s))
-    seen = jnp.concatenate(seen, 0)
+    seen = row_major(jnp.concatenate(seen, 0))
     vecs = seen.shape[0]
     row_part, col_own = seen[:, :1].reshape(vecs, -1), seen[:, 1:].reshape(vecs, -1)
 

time: 37.9 us -> 37.1 us (0.979)
  waiting for transfers between devices: 11.3 us -> 10.6 us
    ppermute x9, waiting for transfers between devices: 10.1 us -> 9.26 us  [flip(): return lax.ppermute(array, axis, [(d, d ^ step) for d in range(count)])]
    pallas_call x2 -> x3, Pallas kernels: 0.83 us -> 1.04 us  [project(): pl.pallas_call(functools.partial(project_kernel, len(lefts), steps), out_...]
  transfers between devices with their start and end apart: 12 -> 12, of which waited for: 7 -> 9; matrix products, arithmetic and copies ran while one was open for 10% -> 10% of each run, Pallas kernels for 5% -> 6%
where the time goes in v3:
time: 37.1 us; the launch traced here: 36.9 us
  starting transfers between devices  13.9 us (37%)
  waiting for transfers between devices  10.6 us (29%)
  Pallas kernels  8.29 us (22%)
  matrix products  3.77 us (10%)
    ppermute x9, starting transfers between devices, flip(): return lax.ppermute(array, axis, [(d, d ^ step) for d in range(count)])  13.7 us
    ppermute x9, waiting for transfers between devices, flip(): return lax.ppermute(array, axis, [(d, d ^ step) for d in range(count)])  9.26 us
    pallas_call x1, Pallas kernels, rest_product(): pl.pallas_call(functools.partial(rest_kernel, side, rows // BLOCKS), out_...  5.93 us
    dot_general x1, matrix products, body(): jnp.einsum('ri,prk->pki', coeffs, cholesky, preferred_element_type=jnp.fl...  3.77 us
    pallas_call x1, Pallas kernels, head_product(): pl.pallas_call(functools.partial(head_kernel, rows // BLOCKS), out_shape=...  1.31 us
    ppermute x1, waiting for transfers between devices, body(): lax.ppermute(lax.dynamic_index_in_dim(partial, 1 - core, 2, keepdims=Fals...  1.24 us
    pallas_call x3, Pallas kernels, project(): pl.pallas_call(functools.partial(project_kernel, len(lefts), steps), out_...  1.04 us
  transfers between devices with their start and end apart: 12, of which 9 were waited for; matrix products, arithmetic and copies ran while one was open for 10% of the time, Pallas kernels for 6%

profile of v3, /device:TPU:0, one launch (start us, length us, event | category | flops | bytes accessed | tf_op | source)
XLA Modules:
  0.0 36.9 jit_solution(10790013594710607853)
XLA Ops:
  0.0 0.0 copy-start
  0.0 5.0 %collective-permute-start.3 = (bf16[384,128]{1,0:T(8,128)(2,1)}, bf16[384,128]{1,0:T(8,128)(2,1)S(1)}, u32[]{:S(2)}, u32[]{:S(2)}) collective-permute-start(bf16[384,128]{1,0:T(8,128)(2,1)} %refs_1_.3), channel_id=1, source_target_pairs={{0,24},{8,16},{16,8},{24,0},{1,25},{9,17},{17,9},{25,1},{2,26},{10... | collective-permute-start | bytes 294920 | tf_op jit(solution)/shard_map/ppermute | solution.py:27
  5.1 0.0 collective-permute-start.2
  5.1 0.6 %collective-permute-start.1 = (bf16[384,128]{1,0:T(8,128)(2,1)}, bf16[384,128]{1,0:T(8,128)(2,1)S(1)}, u32[]{:S(2)}, u32[]{:S(2)}) collective-permute-start(bf16[384,128]{1,0:T(8,128)(2,1)} %refs_1_.3), channel_id=1, source_target_pairs={{0,16},{8,24},{16,0},{24,8},{1,17},{9,25},{17,1},{25,9},{2,18},{10... | collective-permute-start | bytes 294920 | tf_op jit(solution)/shard_map/ppermute | solution.py:27
  5.7 3.8 %convolution_convert_fusion = bf16[2,3072,128]{2,1,0:T(8,128)(2,1)S(1)} fusion(bf16[2,384,3072]{2,1,0:T(8,128)(2,1)} %param.2, bf16[384,128]{1,0:T(8,128)(2,1)} %refs_1_.3), kind=kOutput, calls=%fused_computation | convolution fusion | flops 604766208 | bytes 6389760 | tf_op jit(solution)/shard_map/ri,prk->pki/dot_general | solution.py:173
  9.5 0.1 constant_dynamic-slice_fusion.5
  9.5 0.1 collective-permute-start
  9.6 0.0 collective-permute-done.3.refs_3_
  9.6 1.8 %collective-permute-done.2.refs_2_ = bf16[384,128]{1,0:T(8,128)(2,1)S(1)} collective-permute-done((bf16[384,128]{1,0:T(8,128)(2,1)}, bf16[384,128]{1,0:T(8,128)(2,1)S(1)}, u32[]{:S(2)}, u32[]{:S(2)}) %collective-permute-start.2) | collective-permute-done | bytes 98336 | tf_op jit(solution)/shard_map/ppermute | solution.py:27
  11.4 0.0 copy-done
  11.4 0.4 shard_map.28.refs_4_
  11.8 0.1 collective-permute-done.refs_0_.refs_1_
  11.9 0.4 shard_map.29.refs_3_
  12.2 1.3 %collective-permute-done.1.refs_2_ = bf16[384,128]{1,0:T(8,128)(2,1)S(1)} collective-permute-done((bf16[384,128]{1,0:T(8,128)(2,1)}, bf16[384,128]{1,0:T(8,128)(2,1)S(1)}, u32[]{:S(2)}, u32[]{:S(2)}) %collective-permute-start.1) | collective-permute-done | bytes 98336 | tf_op jit(solution)/shard_map/ppermute | solution.py:27
  13.5 0.3 shard_map.30
  13.9 0.1 collective-permute-start.4
  14.0 1.2 %collective-permute-done.4 = f32[2,4,16,128]{3,2,1,0:T(8,128)S(1)} collective-permute-done((f32[2,4,16,128]{3,2,1,0:T(8,128)S(1)}, f32[2,4,16,128]{3,2,1,0:T(8,128)S(1)}, u32[]{:S(2)}, u32[]{:S(2)}) %collective-permute-start.4) | collective-permute-done | bytes 65568 | tf_op jit(solution)/shard_map/ppermute | solution.py:186
  15.2 2.6 %collective-permute-start.7 = (bf16[2,4,16,128]{3,2,1,0:T(8,128)(2,1)S(1)}, bf16[2,4,16,128]{3,2,1,0:T(8,128)(2,1)S(1)}, u32[]{:S(2)}, u32[]{:S(2)}) collective-permute-start(bf16[2,4,16,128]{3,2,1,0:T(8,128)(2,1)S(1)} %fusion.1), channel_id=1, source_target_pairs={{0,24},{8,16},{16,8},{24,0},{1,25},{9,17},{17,9},{25,1},{2,26},{10... | collective-permute-start | bytes 98312 | tf_op jit(solution)/shard_map/ppermute | solution.py:27
  17.8 0.0 collective-permute-start.6
  17.8 1.8 %collective-permute-start.5 = (bf16[2,4,16,128]{3,2,1,0:T(8,128)(2,1)S(1)}, bf16[2,4,16,128]{3,2,1,0:T(8,128)(2,1)S(1)}, u32[]{:S(2)}, u32[]{:S(2)}) collective-permute-start(bf16[2,4,16,128]{3,2,1,0:T(8,128)(2,1)S(1)} %fusion.1), channel_id=1, source_target_pairs={{0,8},{8,0},{16,24},{24,16},{1,9},{9,1},{17,25},{25,17},{2,10},{10... | collective-permute-start | bytes 98312 | tf_op jit(solution)/shard_map/ppermute | solution.py:27
  19.7 1.3 %collective-permute-done.7 = bf16[2,4,16,128]{3,2,1,0:T(8,128)(2,1)S(1)} collective-permute-done((bf16[2,4,16,128]{3,2,1,0:T(8,128)(2,1)S(1)}, bf16[2,4,16,128]{3,2,1,0:T(8,128)(2,1)S(1)}, u32[]{:S(2)}, u32[]{:S(2)}) %collective-permute-start.7) | collective-permute-done | bytes 32800 | tf_op jit(solution)/shard_map/ppermute | solution.py:27
  21.0 1.6 %collective-permute-done.6 = bf16[2,4,16,128]{3,2,1,0:T(8,128)(2,1)S(1)} collective-permute-done((bf16[2,4,16,128]{3,2,1,0:T(8,128)(2,1)S(1)}, bf16[2,4,16,128]{3,2,1,0:T(8,128)(2,1)S(1)}, u32[]{:S(2)}, u32[]{:S(2)}) %collective-permute-start.6) | collective-permute-done | bytes 32800 | tf_op jit(solution)/shard_map/ppermute | solution.py:27
  22.7 0.0 collective-permute-done.5
  22.7 2.5 %collective-permute-start.8 = (bf16[2,2,16,128]{3,2,1,0:T(8,128)(2,1)S(1)}, bf16[2,2,16,128]{3,2,1,0:T(8,128)(2,1)S(1)}, u32[]{:S(2)}, u32[]{:S(2)}) collective-permute-start(bf16[2,2,16,128]{3,2,1,0:T(8,128)(2,1)S(1)} %get-tuple-element.17), channel_id=1, source_target_pairs={{0,3},{1,2},{2,1},{3,0},{4,7},{5,6},{6,5},{7,4},{8,11},{9,10},{10,... | collective-permute-start | bytes 49160 | tf_op jit(solution)/shard_map/ppermute | solution.py:27
  25.2 0.5 %collective-permute-start.9 = (bf16[2,2,16,128]{3,2,1,0:T(8,128)(2,1)S(1)}, bf16[2,2,16,128]{3,2,1,0:T(8,128)(2,1)S(1)}, u32[]{:S(2)}, u32[]{:S(2)}) collective-permute-start(bf16[2,2,16,128]{3,2,1,0:T(8,128)(2,1)S(1)} %get-tuple-element.18), channel_id=1, source_target_pairs={{0,2},{1,3},{2,0},{3,1},{4,6},{5,7},{6,4},{7,5},{8,10},{9,11},{10,... | collective-permute-start | bytes 49160 | tf_op jit(solution)/shard_map/ppermute | solution.py:27
  25.7 0.5 %collective-permute-start.10 = (bf16[2,2,16,128]{3,2,1,0:T(8,128)(2,1)S(1)}, bf16[2,2,16,128]{3,2,1,0:T(8,128)(2,1)S(1)}, u32[]{:S(2)}, u32[]{:S(2)}) collective-permute-start(bf16[2,2,16,128]{3,2,1,0:T(8,128)(2,1)S(1)} %get-tuple-element.19), channel_id=1, source_target_pairs={{0,1},{1,0},{2,3},{3,2},{4,5},{5,4},{6,7},{7,6},{8,9},{9,8},{10,11... | collective-permute-start | bytes 49160 | tf_op jit(solution)/shard_map/ppermute | solution.py:27
  26.3 1.1 %collective-permute-done.8 = bf16[2,2,16,128]{3,2,1,0:T(8,128)(2,1)S(1)} collective-permute-done((bf16[2,2,16,128]{3,2,1,0:T(8,128)(2,1)S(1)}, bf16[2,2,16,128]{3,2,1,0:T(8,128)(2,1)S(1)}, u32[]{:S(2)}, u32[]{:S(2)}) %collective-permute-start.8) | collective-permute-done | bytes 16416 | tf_op jit(solution)/shard_map/ppermute | solution.py:27
  27.4 1.5 %collective-permute-done.9 = bf16[2,2,16,128]{3,2,1,0:T(8,128)(2,1)S(1)} collective-permute-done((bf16[2,2,16,128]{3,2,1,0:T(8,128)(2,1)S(1)}, bf16[2,2,16,128]{3,2,1,0:T(8,128)(2,1)S(1)}, u32[]{:S(2)}, u32[]{:S(2)}) %collective-permute-start.9) | collective-permute-done | bytes 16416 | tf_op jit(solution)/shard_map/ppermute | solution.py:27
  29.0 0.5 %collective-permute-done.10 = bf16[2,2,16,128]{3,2,1,0:T(8,128)(2,1)S(1)} collective-permute-done((bf16[2,2,16,128]{3,2,1,0:T(8,128)(2,1)S(1)}, bf16[2,2,16,128]{3,2,1,0:T(8,128)(2,1)S(1)}, u32[]{:S(2)}, u32[]{:S(2)}) %collective-permute-start.10) | collective-permute-done | bytes 16416 | tf_op jit(solution)/shard_map/ppermute | solution.py:27
  29.5 0.1 collective-permute-start.11
  29.6 1.3 %shard_map.31 = (bf16[1024,2048]{1,0:T(8,128)(2,1)S(1)}, bf16[2048,8]{1,0:T(8,128)(2,1)S(1)}) custom-call(bf16[8,2048]{1,0:T(8,128)(2,1)S(1)} %get-tuple-element.21.row_ref, bf16[8,2048]{1,0:T(8,128)(2,1)S(1)} %get-tuple-element.20.col_ref.own_ref), custom_call_target="tpu_custom_call" | custom-call | flops 33554432 | bytes 4194304 | tf_op jit(solution)/shard_map/pallas_call | solution.py:129
  30.9 0.0 collective-permute-done.11
  31.0 5.9 %shard_map.32 = bf16[2048,4096]{1,0:T(8,128)(2,1)} custom-call(bf16[1024,2048]{1,0:T(8,128)(2,1)S(1)} %get-tuple-element.7.head_ref, bf16[2048,8]{1,0:T(8,128)(2,1)S(1)} %get-tuple-element.8.flipped_ref, bf16[8,2048]{1,0:T(8,128)(2,1)S(1)} %get-tuple-element.20.col_ref.own_ref, bf16[8,2048]{1,0:T(8,128)(2,1)S(1)} %bitcast.39), custom_call_target="tpu_custom_call" | custom-call | flops 100663296 | bytes 16777216 | tf_op jit(solution)/shard_map/pallas_call | solution.py:148
  (9 shorter events, 0.1 us)
Async XLA Ops:
  0.0 11.4 %copy-start = (bf16[384,128]{1,0:T(8,128)(2,1)S(1)}, bf16[384,128]{1,0:T(8,128)(2,1)}, u32[]{:S(2)}) copy-start(bf16[384,128]{1,0:T(8,128)(2,1)} %refs_1_.3) | copy-start | bytes 294916
  0.0 9.6 %collective-permute-start.3 = (bf16[384,128]{1,0:T(8,128)(2,1)}, bf16[384,128]{1,0:T(8,128)(2,1)S(1)}, u32[]{:S(2)}, u32[]{:S(2)}) collective-permute-start(bf16[384,128]{1,0:T(8,128)(2,1)} %refs_1_.3), channel_id=1, source_target_pairs={{0,24},{8,16},{16,8},{24,0},{1,25},{9,17},{17,9},{25,1},{2,26},{10... | collective-permute-start | bytes 294920 | tf_op jit(solution)/shard_map/ppermute | solution.py:27
  5.1 6.4 %collective-permute-start.2 = (bf16[384,128]{1,0:T(8,128)(2,1)}, bf16[384,128]{1,0:T(8,128)(2,1)S(1)}, u32[]{:S(2)}, u32[]{:S(2)}) collective-permute-start(bf16[384,128]{1,0:T(8,128)(2,1)} %refs_1_.3), channel_id=1, source_target_pairs={{0,8},{8,0},{16,24},{24,16},{1,9},{9,1},{17,25},{25,17},{2,10},{10... | collective-permute-start | bytes 294920 | tf_op jit(solution)/shard_map/ppermute | solution.py:27
  5.1 8.5 %collective-permute-start.1 = (bf16[384,128]{1,0:T(8,128)(2,1)}, bf16[384,128]{1,0:T(8,128)(2,1)S(1)}, u32[]{:S(2)}, u32[]{:S(2)}) collective-permute-start(bf16[384,128]{1,0:T(8,128)(2,1)} %refs_1_.3), channel_id=1, source_target_pairs={{0,16},{8,24},{16,0},{24,8},{1,17},{9,25},{17,1},{25,9},{2,18},{10... | collective-permute-start | bytes 294920 | tf_op jit(solution)/shard_map/ppermute | solution.py:27
  9.5 2.4 %collective-permute-start = (bf16[2,4,1,384,128]{4,3,2,1,0:T(8,128)(2,1)S(1)}, bf16[2,4,1,384,128]{4,3,2,1,0:T(8,128)(2,1)S(1)}, u32[]{:S(2)}, u32[]{:S(2)}) collective-permute-start(bf16[2,4,1,384,128]{4,3,2,1,0:T(8,128)(2,1)S(1)} %constant_dynamic-slice_fusion.5), channel_id=1, source_target_pairs={{0,4},{4,0},{1,5},{5,1},{2,6},{6,2},{3,7},{7,3},{8,12},{12,8},{9,1... | collective-permute-start | bytes 2359304 | tf_op jit(solution)/shard_map/ppermute | solution.py:176
  13.9 1.3 %collective-permute-start.4 = (f32[2,4,16,128]{3,2,1,0:T(8,128)S(1)}, f32[2,4,16,128]{3,2,1,0:T(8,128)S(1)}, u32[]{:S(2)}, u32[]{:S(2)}) collective-permute-start(f32[2,4,16,128]{3,2,1,0:T(8,128)S(1)} %dynamic-slice_bitcast_fusion), channel_id=1, source_target_pairs={{0,4},{4,0},{1,5},{5,1},{2,6},{6,2},{3,7},{7,3},{8,12},{12,8},{9,1... | collective-permute-start | bytes 196616 | tf_op jit(solution)/shard_map/ppermute | solution.py:186
  15.2 5.8 %collective-permute-start.7 = (bf16[2,4,16,128]{3,2,1,0:T(8,128)(2,1)S(1)}, bf16[2,4,16,128]{3,2,1,0:T(8,128)(2,1)S(1)}, u32[]{:S(2)}, u32[]{:S(2)}) collective-permute-start(bf16[2,4,16,128]{3,2,1,0:T(8,128)(2,1)S(1)} %fusion.1), channel_id=1, source_target_pairs={{0,24},{8,16},{16,8},{24,0},{1,25},{9,17},{17,9},{25,1},{2,26},{10... | collective-permute-start | bytes 98312 | tf_op jit(solution)/shard_map/ppermute | solution.py:27
  17.8 4.8 %collective-permute-start.6 = (bf16[2,4,16,128]{3,2,1,0:T(8,128)(2,1)S(1)}, bf16[2,4,16,128]{3,2,1,0:T(8,128)(2,1)S(1)}, u32[]{:S(2)}, u32[]{:S(2)}) collective-permute-start(bf16[2,4,16,128]{3,2,1,0:T(8,128)(2,1)S(1)} %fusion.1), channel_id=1, source_target_pairs={{0,16},{8,24},{16,0},{24,8},{1,17},{9,25},{17,1},{25,9},{2,18},{10... | collective-permute-start | bytes 98312 | tf_op jit(solution)/shard_map/ppermute | solution.py:27
  17.8 4.8 %collective-permute-start.5 = (bf16[2,4,16,128]{3,2,1,0:T(8,128)(2,1)S(1)}, bf16[2,4,16,128]{3,2,1,0:T(8,128)(2,1)S(1)}, u32[]{:S(2)}, u32[]{:S(2)}) collective-permute-start(bf16[2,4,16,128]{3,2,1,0:T(8,128)(2,1)S(1)} %fusion.1), channel_id=1, source_target_pairs={{0,8},{8,0},{16,24},{24,16},{1,9},{9,1},{17,25},{25,17},{2,10},{10... | collective-permute-start | bytes 98312 | tf_op jit(solution)/shard_map/ppermute | solution.py:27
  22.7 4.7 %collective-permute-start.8 = (bf16[2,2,16,128]{3,2,1,0:T(8,128)(2,1)S(1)}, bf16[2,2,16,128]{3,2,1,0:T(8,128)(2,1)S(1)}, u32[]{:S(2)}, u32[]{:S(2)}) collective-permute-start(bf16[2,2,16,128]{3,2,1,0:T(8,128)(2,1)S(1)} %get-tuple-element.17), channel_id=1, source_target_pairs={{0,3},{1,2},{2,1},{3,0},{4,7},{5,6},{6,5},{7,4},{8,11},{9,10},{10,... | collective-permute-start | bytes 49160 | tf_op jit(solution)/shard_map/ppermute | solution.py:27
  25.2 3.7 %collective-permute-start.9 = (bf16[2,2,16,128]{3,2,1,0:T(8,128)(2,1)S(1)}, bf16[2,2,16,128]{3,2,1,0:T(8,128)(2,1)S(1)}, u32[]{:S(2)}, u32[]{:S(2)}) collective-permute-start(bf16[2,2,16,128]{3,2,1,0:T(8,128)(2,1)S(1)} %get-tuple-element.18), channel_id=1, source_target_pairs={{0,2},{1,3},{2,0},{3,1},{4,6},{5,7},{6,4},{7,5},{8,10},{9,11},{10,... | collective-permute-start | bytes 49160 | tf_op jit(solution)/shard_map/ppermute | solution.py:27
  25.7 3.7 %collective-permute-start.10 = (bf16[2,2,16,128]{3,2,1,0:T(8,128)(2,1)S(1)}, bf16[2,2,16,128]{3,2,1,0:T(8,128)(2,1)S(1)}, u32[]{:S(2)}, u32[]{:S(2)}) collective-permute-start(bf16[2,2,16,128]{3,2,1,0:T(8,128)(2,1)S(1)} %get-tuple-element.19), channel_id=1, source_target_pairs={{0,1},{1,0},{2,3},{3,2},{4,5},{5,4},{6,7},{7,6},{8,9},{9,8},{10,11... | collective-permute-start | bytes 49160 | tf_op jit(solution)/shard_map/ppermute | solution.py:27
  29.5 1.4 %collective-permute-start.11 = (bf16[8,1,16,128]{3,2,1,0:T(8,128)(2,1)S(1)}, bf16[8,1,16,128]{3,2,1,0:T(8,128)(2,1)S(1)}, u32[]{:S(2)}, u32[]{:S(2)}) collective-permute-start(bf16[8,1,16,128]{3,2,1,0:T(8,128)(2,1)S(1)} %get-tuple-element.9), channel_id=1, source_target_pairs={{0,4},{4,0},{1,5},{5,1},{2,6},{6,2},{3,7},{7,3},{8,12},{12,8},{9,1... | collective-permute-start | bytes 98312 | tf_op jit(solution)/shard_map/ppermute | solution.py:203

commit v4 on v3

--- a/solution.py
+++ b/solution.py
@@ -9,7 +9,7 @@
 from jax.sharding import Mesh, PartitionSpec as P
 
 CORES = 2
-LAST = 2
+LATE = (1, 2)
 AO = ("z", "core")
 SWAP = [(0, 1), (1, 0)]
 
@@ -174,11 +174,11 @@
     left = left.astype(jnp.bfloat16).reshape(vec_dev, nz, CORES, rows, orbitals)
     give = lax.dynamic_slice_in_dim(left, 1 - core, 1, 2)
     got = lax.ppermute(give, "core", SWAP)
-    late = LAST % nz
-    steps = [s for s in range(nz) if s != late]
+    late = [s for s in LATE if s < nz]
+    steps = [s for s in range(nz) if s not in late]
     partial = project([left], held, steps, flops=10**11)
     partial = project([got], held, steps, partial)
-    partial = project([left, got], held, [late], partial)
+    partial = project([left, got], held, late, partial)
 
     span = orbitals // (nz * CORES)
     partial = partial.reshape(vec_dev, nz, CORES, span, orbitals)

time: 37.1 us -> 37.1 us (level)
    ppermute x1, waiting for transfers between devices: 0.1 us -> 1.92 us  [body(): got = lax.ppermute(give, 'core', SWAP)]
    ppermute x9, waiting for transfers between devices: 9.26 us -> 7.46 us  [flip(): return lax.ppermute(array, axis, [(d, d ^ step) for d in range(count)])]
  transfers between devices with their start and end apart: 12 -> 12, of which waited for: 9 -> 8; matrix products, arithmetic and copies ran while one was open for 10% -> 10% of each run, Pallas kernels for 6% -> 5%
where the time goes in v4:
time: 37.1 us; the launch traced here: 36.9 us
  starting transfers between devices  13.9 us (37%)
  waiting for transfers between devices  10.6 us (29%)
  Pallas kernels  8.3 us (22%)
  matrix products  3.77 us (10%)
    ppermute x9, starting transfers between devices, flip(): return lax.ppermute(array, axis, [(d, d ^ step) for d in range(count)])  13.7 us
    ppermute x9, waiting for transfers between devices, flip(): return lax.ppermute(array, axis, [(d, d ^ step) for d in range(count)])  7.46 us
    pallas_call x1, Pallas kernels, rest_product(): pl.pallas_call(functools.partial(rest_kernel, side, rows // BLOCKS), out_...  5.93 us
    dot_general x1, matrix products, body(): jnp.einsum('ri,prk->pki', coeffs, cholesky, preferred_element_type=jnp.fl...  3.77 us
    ppermute x1, waiting for transfers between devices, body(): got = lax.ppermute(give, 'core', SWAP)  1.92 us
    pallas_call x1, Pallas kernels, head_product(): pl.pallas_call(functools.partial(head_kernel, rows // BLOCKS), out_shape=...  1.31 us
    ppermute x1, waiting for transfers between devices, body(): lax.ppermute(lax.dynamic_index_in_dim(partial, 1 - core, 2, keepdims=Fals...  1.24 us
    pallas_call x3, Pallas kernels, project(): pl.pallas_call(functools.partial(project_kernel, len(lefts), steps), out_...  1.06 us
  transfers between devices with their start and end apart: 12, of which 8 were waited for; matrix products, arithmetic and copies ran while one was open for 10% of the time, Pallas kernels for 5%

profile of v4, /device:TPU:0, one launch (start us, length us, event | category | flops | bytes accessed | tf_op | source)
XLA Modules:
  0.0 36.9 jit_solution(17800222725142915414)
XLA Ops:
  0.0 0.0 copy-start
  0.0 5.0 %collective-permute-start.3 = (bf16[384,128]{1,0:T(8,128)(2,1)}, bf16[384,128]{1,0:T(8,128)(2,1)S(1)}, u32[]{:S(2)}, u32[]{:S(2)}) collective-permute-start(bf16[384,128]{1,0:T(8,128)(2,1)} %refs_1_.3), channel_id=1, source_target_pairs={{0,24},{8,16},{16,8},{24,0},{1,25},{9,17},{17,9},{25,1},{2,26},{10... | collective-permute-start | bytes 294920 | tf_op jit(solution)/shard_map/ppermute | solution.py:27
  5.1 0.0 collective-permute-start.2
  5.1 0.6 %collective-permute-start.1 = (bf16[384,128]{1,0:T(8,128)(2,1)}, bf16[384,128]{1,0:T(8,128)(2,1)S(1)}, u32[]{:S(2)}, u32[]{:S(2)}) collective-permute-start(bf16[384,128]{1,0:T(8,128)(2,1)} %refs_1_.3), channel_id=1, source_target_pairs={{0,8},{8,0},{16,24},{24,16},{1,9},{9,1},{17,25},{25,17},{2,10},{10... | collective-permute-start | bytes 294920 | tf_op jit(solution)/shard_map/ppermute | solution.py:27
  5.7 3.8 %convolution_convert_fusion = bf16[2,3072,128]{2,1,0:T(8,128)(2,1)S(1)} fusion(bf16[2,384,3072]{2,1,0:T(8,128)(2,1)} %param.2, bf16[384,128]{1,0:T(8,128)(2,1)} %refs_1_.3), kind=kOutput, calls=%fused_computation | convolution fusion | flops 604766208 | bytes 6389760 | tf_op jit(solution)/shard_map/ri,prk->pki/dot_general | solution.py:173
  9.5 0.1 constant_dynamic-slice_fusion.5
  9.5 0.1 collective-permute-start
  9.6 0.0 collective-permute-done.3.refs_2_
  9.6 0.0 copy-done
  9.6 0.3 shard_map.28.refs_3_
  10.0 1.9 %collective-permute-done.refs_0_.refs_1_ = bf16[2,4,1,384,128]{4,3,2,1,0:T(8,128)(2,1)S(1)} collective-permute-done((bf16[2,4,1,384,128]{4,3,2,1,0:T(8,128)(2,1)S(1)}, bf16[2,4,1,384,128]{4,3,2,1,0:T(8,128)(2,1)S(1)}, u32[]{:S(2)}, u32[]{:S(2)}) %collective-permute-start) | collective-permute-done | bytes 786464 | tf_op jit(solution)/shard_map/ppermute | solution.py:176
  11.9 0.3 shard_map.29.refs_4_
  12.2 1.3 %collective-permute-done.2.refs_3_ = bf16[384,128]{1,0:T(8,128)(2,1)S(1)} collective-permute-done((bf16[384,128]{1,0:T(8,128)(2,1)}, bf16[384,128]{1,0:T(8,128)(2,1)S(1)}, u32[]{:S(2)}, u32[]{:S(2)}) %collective-permute-start.2) | collective-permute-done | bytes 98336 | tf_op jit(solution)/shard_map/ppermute | solution.py:27
  13.5 0.0 collective-permute-done.1.refs_2_
  13.5 0.4 %shard_map.30 = f32[2,128,128]{2,1,0:T(8,128)S(1)} custom-call(bf16[2,4,2,384,128]{4,3,2,1,0:T(8,128)(2,1)S(1)} %bitcast.35, bf16[2,4,1,384,128]{4,3,2,1,0:T(8,128)(2,1)S(1)} %collective-permute-done.refs_0_.refs_1_, bf16[384,128]{1,0:T(8,128)(2,1)S(1)} %collective-permute-done.1.refs_2_, bf16[384,128]{1,0:T(8,128)(2,1)S(1)} %collective-permute-done.2.refs_3_, ...), custom_call_target="tpu_custom_call" | custom-call | flops 100663296 | bytes 100663 | tf_op jit(solution)/shard_map/pallas_call | solution.py:51
  14.0 0.1 collective-permute-start.4
  14.1 1.2 %collective-permute-done.4 = f32[2,4,16,128]{3,2,1,0:T(8,128)S(1)} collective-permute-done((f32[2,4,16,128]{3,2,1,0:T(8,128)S(1)}, f32[2,4,16,128]{3,2,1,0:T(8,128)S(1)}, u32[]{:S(2)}, u32[]{:S(2)}) %collective-permute-start.4) | collective-permute-done | bytes 65568 | tf_op jit(solution)/shard_map/ppermute | solution.py:186
  15.3 2.6 %collective-permute-start.7 = (bf16[2,4,16,128]{3,2,1,0:T(8,128)(2,1)S(1)}, bf16[2,4,16,128]{3,2,1,0:T(8,128)(2,1)S(1)}, u32[]{:S(2)}, u32[]{:S(2)}) collective-permute-start(bf16[2,4,16,128]{3,2,1,0:T(8,128)(2,1)S(1)} %fusion.1), channel_id=1, source_target_pairs={{0,24},{8,16},{16,8},{24,0},{1,25},{9,17},{17,9},{25,1},{2,26},{10... | collective-permute-start | bytes 98312 | tf_op jit(solution)/shard_map/ppermute | solution.py:27
  17.9 0.0 collective-permute-start.6
  17.9 1.9 %collective-permute-start.5 = (bf16[2,4,16,128]{3,2,1,0:T(8,128)(2,1)S(1)}, bf16[2,4,16,128]{3,2,1,0:T(8,128)(2,1)S(1)}, u32[]{:S(2)}, u32[]{:S(2)}) collective-permute-start(bf16[2,4,16,128]{3,2,1,0:T(8,128)(2,1)S(1)} %fusion.1), channel_id=1, source_target_pairs={{0,8},{8,0},{16,24},{24,16},{1,9},{9,1},{17,25},{25,17},{2,10},{10... | collective-permute-start | bytes 98312 | tf_op jit(solution)/shard_map/ppermute | solution.py:27
  19.8 1.3 %collective-permute-done.7 = bf16[2,4,16,128]{3,2,1,0:T(8,128)(2,1)S(1)} collective-permute-done((bf16[2,4,16,128]{3,2,1,0:T(8,128)(2,1)S(1)}, bf16[2,4,16,128]{3,2,1,0:T(8,128)(2,1)S(1)}, u32[]{:S(2)}, u32[]{:S(2)}) %collective-permute-start.7) | collective-permute-done | bytes 32800 | tf_op jit(solution)/shard_map/ppermute | solution.py:27
  21.1 1.6 %collective-permute-done.6 = bf16[2,4,16,128]{3,2,1,0:T(8,128)(2,1)S(1)} collective-permute-done((bf16[2,4,16,128]{3,2,1,0:T(8,128)(2,1)S(1)}, bf16[2,4,16,128]{3,2,1,0:T(8,128)(2,1)S(1)}, u32[]{:S(2)}, u32[]{:S(2)}) %collective-permute-start.6) | collective-permute-done | bytes 32800 | tf_op jit(solution)/shard_map/ppermute | solution.py:27
  22.7 0.0 collective-permute-done.5
  22.8 2.5 %collective-permute-start.8 = (bf16[2,2,16,128]{3,2,1,0:T(8,128)(2,1)S(1)}, bf16[2,2,16,128]{3,2,1,0:T(8,128)(2,1)S(1)}, u32[]{:S(2)}, u32[]{:S(2)}) collective-permute-start(bf16[2,2,16,128]{3,2,1,0:T(8,128)(2,1)S(1)} %get-tuple-element.17), channel_id=1, source_target_pairs={{0,3},{1,2},{2,1},{3,0},{4,7},{5,6},{6,5},{7,4},{8,11},{9,10},{10,... | collective-permute-start | bytes 49160 | tf_op jit(solution)/shard_map/ppermute | solution.py:27
  25.3 0.5 %collective-permute-start.9 = (bf16[2,2,16,128]{3,2,1,0:T(8,128)(2,1)S(1)}, bf16[2,2,16,128]{3,2,1,0:T(8,128)(2,1)S(1)}, u32[]{:S(2)}, u32[]{:S(2)}) collective-permute-start(bf16[2,2,16,128]{3,2,1,0:T(8,128)(2,1)S(1)} %get-tuple-element.18), channel_id=1, source_target_pairs={{0,2},{1,3},{2,0},{3,1},{4,6},{5,7},{6,4},{7,5},{8,10},{9,11},{10,... | collective-permute-start | bytes 49160 | tf_op jit(solution)/shard_map/ppermute | solution.py:27
  25.8 0.5 %collective-permute-start.10 = (bf16[2,2,16,128]{3,2,1,0:T(8,128)(2,1)S(1)}, bf16[2,2,16,128]{3,2,1,0:T(8,128)(2,1)S(1)}, u32[]{:S(2)}, u32[]{:S(2)}) collective-permute-start(bf16[2,2,16,128]{3,2,1,0:T(8,128)(2,1)S(1)} %get-tuple-element.19), channel_id=1, source_target_pairs={{0,1},{1,0},{2,3},{3,2},{4,5},{5,4},{6,7},{7,6},{8,9},{9,8},{10,11... | collective-permute-start | bytes 49160 | tf_op jit(solution)/shard_map/ppermute | solution.py:27
  26.3 1.1 %collective-permute-done.8 = bf16[2,2,16,128]{3,2,1,0:T(8,128)(2,1)S(1)} collective-permute-done((bf16[2,2,16,128]{3,2,1,0:T(8,128)(2,1)S(1)}, bf16[2,2,16,128]{3,2,1,0:T(8,128)(2,1)S(1)}, u32[]{:S(2)}, u32[]{:S(2)}) %collective-permute-start.8) | collective-permute-done | bytes 16416 | tf_op jit(solution)/shard_map/ppermute | solution.py:27
  27.5 1.5 %collective-permute-done.9 = bf16[2,2,16,128]{3,2,1,0:T(8,128)(2,1)S(1)} collective-permute-done((bf16[2,2,16,128]{3,2,1,0:T(8,128)(2,1)S(1)}, bf16[2,2,16,128]{3,2,1,0:T(8,128)(2,1)S(1)}, u32[]{:S(2)}, u32[]{:S(2)}) %collective-permute-start.9) | collective-permute-done | bytes 16416 | tf_op jit(solution)/shard_map/ppermute | solution.py:27
  29.0 0.5 %collective-permute-done.10 = bf16[2,2,16,128]{3,2,1,0:T(8,128)(2,1)S(1)} collective-permute-done((bf16[2,2,16,128]{3,2,1,0:T(8,128)(2,1)S(1)}, bf16[2,2,16,128]{3,2,1,0:T(8,128)(2,1)S(1)}, u32[]{:S(2)}, u32[]{:S(2)}) %collective-permute-start.10) | collective-permute-done | bytes 16416 | tf_op jit(solution)/shard_map/ppermute | solution.py:27
  29.6 0.1 collective-permute-start.11
  29.7 1.3 %shard_map.31 = (bf16[1024,2048]{1,0:T(8,128)(2,1)S(1)}, bf16[2048,8]{1,0:T(8,128)(2,1)S(1)}) custom-call(bf16[8,2048]{1,0:T(8,128)(2,1)S(1)} %get-tuple-element.21.row_ref, bf16[8,2048]{1,0:T(8,128)(2,1)S(1)} %get-tuple-element.20.col_ref.own_ref), custom_call_target="tpu_custom_call" | custom-call | flops 33554432 | bytes 4194304 | tf_op jit(solution)/shard_map/pallas_call | solution.py:129
  31.0 0.0 collective-permute-done.11
  31.0 5.9 %shard_map.32 = bf16[2048,4096]{1,0:T(8,128)(2,1)} custom-call(bf16[1024,2048]{1,0:T(8,128)(2,1)S(1)} %get-tuple-element.7.head_ref, bf16[2048,8]{1,0:T(8,128)(2,1)S(1)} %get-tuple-element.8.flipped_ref, bf16[8,2048]{1,0:T(8,128)(2,1)S(1)} %get-tuple-element.20.col_ref.own_ref, bf16[8,2048]{1,0:T(8,128)(2,1)S(1)} %bitcast.39), custom_call_target="tpu_custom_call" | custom-call | flops 100663296 | bytes 16777216 | tf_op jit(solution)/shard_map/pallas_call | solution.py:148
  (9 shorter events, 0.1 us)
Async XLA Ops:
  0.0 9.6 %copy-start = (bf16[384,128]{1,0:T(8,128)(2,1)S(1)}, bf16[384,128]{1,0:T(8,128)(2,1)}, u32[]{:S(2)}) copy-start(bf16[384,128]{1,0:T(8,128)(2,1)} %refs_1_.3) | copy-start | bytes 294916
  0.0 9.6 %collective-permute-start.3 = (bf16[384,128]{1,0:T(8,128)(2,1)}, bf16[384,128]{1,0:T(8,128)(2,1)S(1)}, u32[]{:S(2)}, u32[]{:S(2)}) collective-permute-start(bf16[384,128]{1,0:T(8,128)(2,1)} %refs_1_.3), channel_id=1, source_target_pairs={{0,24},{8,16},{16,8},{24,0},{1,25},{9,17},{17,9},{25,1},{2,26},{10... | collective-permute-start | bytes 294920 | tf_op jit(solution)/shard_map/ppermute | solution.py:27
  5.1 8.5 %collective-permute-start.2 = (bf16[384,128]{1,0:T(8,128)(2,1)}, bf16[384,128]{1,0:T(8,128)(2,1)S(1)}, u32[]{:S(2)}, u32[]{:S(2)}) collective-permute-start(bf16[384,128]{1,0:T(8,128)(2,1)} %refs_1_.3), channel_id=1, source_target_pairs={{0,16},{8,24},{16,0},{24,8},{1,17},{9,25},{17,1},{25,9},{2,18},{10... | collective-permute-start | bytes 294920 | tf_op jit(solution)/shard_map/ppermute | solution.py:27
  5.1 8.5 %collective-permute-start.1 = (bf16[384,128]{1,0:T(8,128)(2,1)}, bf16[384,128]{1,0:T(8,128)(2,1)S(1)}, u32[]{:S(2)}, u32[]{:S(2)}) collective-permute-start(bf16[384,128]{1,0:T(8,128)(2,1)} %refs_1_.3), channel_id=1, source_target_pairs={{0,8},{8,0},{16,24},{24,16},{1,9},{9,1},{17,25},{25,17},{2,10},{10... | collective-permute-start | bytes 294920 | tf_op jit(solution)/shard_map/ppermute | solution.py:27
  9.5 2.4 %collective-permute-start = (bf16[2,4,1,384,128]{4,3,2,1,0:T(8,128)(2,1)S(1)}, bf16[2,4,1,384,128]{4,3,2,1,0:T(8,128)(2,1)S(1)}, u32[]{:S(2)}, u32[]{:S(2)}) collective-permute-start(bf16[2,4,1,384,128]{4,3,2,1,0:T(8,128)(2,1)S(1)} %constant_dynamic-slice_fusion.5), channel_id=1, source_target_pairs={{0,4},{4,0},{1,5},{5,1},{2,6},{6,2},{3,7},{7,3},{8,12},{12,8},{9,1... | collective-permute-start | bytes 2359304 | tf_op jit(solution)/shard_map/ppermute | solution.py:176
  14.0 1.3 %collective-permute-start.4 = (f32[2,4,16,128]{3,2,1,0:T(8,128)S(1)}, f32[2,4,16,128]{3,2,1,0:T(8,128)S(1)}, u32[]{:S(2)}, u32[]{:S(2)}) collective-permute-start(f32[2,4,16,128]{3,2,1,0:T(8,128)S(1)} %dynamic-slice_bitcast_fusion), channel_id=1, source_target_pairs={{0,4},{4,0},{1,5},{5,1},{2,6},{6,2},{3,7},{7,3},{8,12},{12,8},{9,1... | collective-permute-start | bytes 196616 | tf_op jit(solution)/shard_map/ppermute | solution.py:186
  15.3 5.8 %collective-permute-start.7 = (bf16[2,4,16,128]{3,2,1,0:T(8,128)(2,1)S(1)}, bf16[2,4,16,128]{3,2,1,0:T(8,128)(2,1)S(1)}, u32[]{:S(2)}, u32[]{:S(2)}) collective-permute-start(bf16[2,4,16,128]{3,2,1,0:T(8,128)(2,1)S(1)} %fusion.1), channel_id=1, source_target_pairs={{0,24},{8,16},{16,8},{24,0},{1,25},{9,17},{17,9},{25,1},{2,26},{10... | collective-permute-start | bytes 98312 | tf_op jit(solution)/shard_map/ppermute | solution.py:27
  17.9 4.8 %collective-permute-start.6 = (bf16[2,4,16,128]{3,2,1,0:T(8,128)(2,1)S(1)}, bf16[2,4,16,128]{3,2,1,0:T(8,128)(2,1)S(1)}, u32[]{:S(2)}, u32[]{:S(2)}) collective-permute-start(bf16[2,4,16,128]{3,2,1,0:T(8,128)(2,1)S(1)} %fusion.1), channel_id=1, source_target_pairs={{0,16},{8,24},{16,0},{24,8},{1,17},{9,25},{17,1},{25,9},{2,18},{10... | collective-permute-start | bytes 98312 | tf_op jit(solution)/shard_map/ppermute | solution.py:27
  17.9 4.8 %collective-permute-start.5 = (bf16[2,4,16,128]{3,2,1,0:T(8,128)(2,1)S(1)}, bf16[2,4,16,128]{3,2,1,0:T(8,128)(2,1)S(1)}, u32[]{:S(2)}, u32[]{:S(2)}) collective-permute-start(bf16[2,4,16,128]{3,2,1,0:T(8,128)(2,1)S(1)} %fusion.1), channel_id=1, source_target_pairs={{0,8},{8,0},{16,24},{24,16},{1,9},{9,1},{17,25},{25,17},{2,10},{10... | collective-permute-start | bytes 98312 | tf_op jit(solution)/shard_map/ppermute | solution.py:27
  22.8 4.7 %collective-permute-start.8 = (bf16[2,2,16,128]{3,2,1,0:T(8,128)(2,1)S(1)}, bf16[2,2,16,128]{3,2,1,0:T(8,128)(2,1)S(1)}, u32[]{:S(2)}, u32[]{:S(2)}) collective-permute-start(bf16[2,2,16,128]{3,2,1,0:T(8,128)(2,1)S(1)} %get-tuple-element.17), channel_id=1, source_target_pairs={{0,3},{1,2},{2,1},{3,0},{4,7},{5,6},{6,5},{7,4},{8,11},{9,10},{10,... | collective-permute-start | bytes 49160 | tf_op jit(solution)/shard_map/ppermute | solution.py:27
  25.3 3.7 %collective-permute-start.9 = (bf16[2,2,16,128]{3,2,1,0:T(8,128)(2,1)S(1)}, bf16[2,2,16,128]{3,2,1,0:T(8,128)(2,1)S(1)}, u32[]{:S(2)}, u32[]{:S(2)}) collective-permute-start(bf16[2,2,16,128]{3,2,1,0:T(8,128)(2,1)S(1)} %get-tuple-element.18), channel_id=1, source_target_pairs={{0,2},{1,3},{2,0},{3,1},{4,6},{5,7},{6,4},{7,5},{8,10},{9,11},{10,... | collective-permute-start | bytes 49160 | tf_op jit(solution)/shard_map/ppermute | solution.py:27
  25.8 3.7 %collective-permute-start.10 = (bf16[2,2,16,128]{3,2,1,0:T(8,128)(2,1)S(1)}, bf16[2,2,16,128]{3,2,1,0:T(8,128)(2,1)S(1)}, u32[]{:S(2)}, u32[]{:S(2)}) collective-permute-start(bf16[2,2,16,128]{3,2,1,0:T(8,128)(2,1)S(1)} %get-tuple-element.19), channel_id=1, source_target_pairs={{0,1},{1,0},{2,3},{3,2},{4,5},{5,4},{6,7},{7,6},{8,9},{9,8},{10,11... | collective-permute-start | bytes 49160 | tf_op jit(solution)/shard_map/ppermute | solution.py:27
  29.6 1.4 %collective-permute-start.11 = (bf16[8,1,16,128]{3,2,1,0:T(8,128)(2,1)S(1)}, bf16[8,1,16,128]{3,2,1,0:T(8,128)(2,1)S(1)}, u32[]{:S(2)}, u32[]{:S(2)}) collective-permute-start(bf16[8,1,16,128]{3,2,1,0:T(8,128)(2,1)S(1)} %get-tuple-element.9), channel_id=1, source_target_pairs={{0,4},{4,0},{1,5},{5,1},{2,6},{6,2},{3,7},{7,3},{8,12},{12,8},{9,1... | collective-permute-start | bytes 98312 | tf_op jit(solution)/shard_map/ppermute | solution.py:203

commit v5 on v4

--- a/solution.py
+++ b/solution.py
@@ -9,7 +9,7 @@
 from jax.sharding import Mesh, PartitionSpec as P
 
 CORES = 2
-LATE = (1, 2)
+LATE = (1, 3)
 AO = ("z", "core")
 SWAP = [(0, 1), (1, 0)]
 

time: 37.1 us -> 37.4 us (level)
    ppermute x9, waiting for transfers between devices: 7.46 us -> 9.66 us  [flip(): return lax.ppermute(array, axis, [(d, d ^ step) for d in range(count)])]
    ppermute x1, waiting for transfers between devices: 1.92 us -> 0.01 us  [body(): got = lax.ppermute(give, 'core', SWAP)]
  transfers between devices with their start and end apart: 12 -> 12, of which waited for: 8 -> 7; matrix products, arithmetic and copies ran while one was open for 10% -> 10% of each run, Pallas kernels for 5% -> 5%
where the time goes in v5:
time: 37.4 us; the launch traced here: 37.2 us
  starting transfers between devices  13.8 us (37%)
  waiting for transfers between devices  10.9 us (29%)
  Pallas kernels  8.31 us (22%)
  matrix products  3.77 us (10%)
    ppermute x9, starting transfers between devices, flip(): return lax.ppermute(array, axis, [(d, d ^ step) for d in range(count)])  13.6 us
    ppermute x9, waiting for transfers between devices, flip(): return lax.ppermute(array, axis, [(d, d ^ step) for d in range(count)])  9.66 us
    pallas_call x1, Pallas kernels, rest_product(): pl.pallas_call(functools.partial(rest_kernel, side, rows // BLOCKS), out_...  5.93 us
    dot_general x1, matrix products, body(): jnp.einsum('ri,prk->pki', coeffs, cholesky, preferred_element_type=jnp.fl...  3.77 us
    pallas_call x1, Pallas kernels, head_product(): pl.pallas_call(functools.partial(head_kernel, rows // BLOCKS), out_shape=...  1.31 us
    ppermute x1, waiting for transfers between devices, body(): lax.ppermute(lax.dynamic_index_in_dim(partial, 1 - core, 2, keepdims=Fals...  1.24 us
    pallas_call x3, Pallas kernels, project(): pl.pallas_call(functools.partial(project_kernel, len(lefts), steps), out_...  1.06 us
  transfers between devices with their start and end apart: 12, of which 7 were waited for; matrix products, arithmetic and copies ran while one was open for 10% of the time, Pallas kernels for 5%

profile of v5, /device:TPU:0, one launch (start us, length us, event | category | flops | bytes accessed | tf_op | source)
XLA Modules:
  0.0 37.2 jit_solution(4389125485290951330)
XLA Ops:
  0.0 0.0 copy-start
  0.0 4.0 %collective-permute-start.3 = (bf16[384,128]{1,0:T(8,128)(2,1)}, bf16[384,128]{1,0:T(8,128)(2,1)S(1)}, u32[]{:S(2)}, u32[]{:S(2)}) collective-permute-start(bf16[384,128]{1,0:T(8,128)(2,1)} %refs_1_.3), channel_id=1, source_target_pairs={{0,16},{8,24},{16,0},{24,8},{1,17},{9,25},{17,1},{25,9},{2,18},{10... | collective-permute-start | bytes 294920 | tf_op jit(solution)/shard_map/ppermute | solution.py:27
  4.0 1.3 %collective-permute-start.2 = (bf16[384,128]{1,0:T(8,128)(2,1)}, bf16[384,128]{1,0:T(8,128)(2,1)S(1)}, u32[]{:S(2)}, u32[]{:S(2)}) collective-permute-start(bf16[384,128]{1,0:T(8,128)(2,1)} %refs_1_.3), channel_id=1, source_target_pairs={{0,24},{8,16},{16,8},{24,0},{1,25},{9,17},{17,9},{25,1},{2,26},{10... | collective-permute-start | bytes 294920 | tf_op jit(solution)/shard_map/ppermute | solution.py:27
  5.4 0.2 collective-permute-start.1
  5.6 3.8 %convolution_convert_fusion = bf16[2,3072,128]{2,1,0:T(8,128)(2,1)S(1)} fusion(bf16[2,384,3072]{2,1,0:T(8,128)(2,1)} %param.2, bf16[384,128]{1,0:T(8,128)(2,1)} %refs_1_.3), kind=kOutput, calls=%fused_computation | convolution fusion | flops 604766208 | bytes 6389760 | tf_op jit(solution)/shard_map/ri,prk->pki/dot_general | solution.py:173
  9.4 0.1 constant_dynamic-slice_fusion.5
  9.5 0.1 collective-permute-start
  9.5 2.7 %collective-permute-done.3.refs_2_ = bf16[384,128]{1,0:T(8,128)(2,1)S(1)} collective-permute-done((bf16[384,128]{1,0:T(8,128)(2,1)}, bf16[384,128]{1,0:T(8,128)(2,1)S(1)}, u32[]{:S(2)}, u32[]{:S(2)}) %collective-permute-start.3) | collective-permute-done | bytes 98336 | tf_op jit(solution)/shard_map/ppermute | solution.py:27
  12.2 0.0 copy-done
  12.2 0.3 shard_map.28.refs_3_
  12.5 0.0 collective-permute-done.refs_0_.refs_1_
  12.5 0.3 shard_map.29.refs_4_
  12.9 0.0 collective-permute-done.2.refs_3_
  12.9 0.0 collective-permute-done.1.refs_2_
  12.9 0.4 %shard_map.30 = f32[2,128,128]{2,1,0:T(8,128)S(1)} custom-call(bf16[2,4,2,384,128]{4,3,2,1,0:T(8,128)(2,1)S(1)} %bitcast.35, bf16[2,4,1,384,128]{4,3,2,1,0:T(8,128)(2,1)S(1)} %collective-permute-done.refs_0_.refs_1_, bf16[384,128]{1,0:T(8,128)(2,1)S(1)} %collective-permute-done.1.refs_2_, bf16[384,128]{1,0:T(8,128)(2,1)S(1)} %collective-permute-done.2.refs_3_, ...), custom_call_target="tpu_custom_call" | custom-call | flops 100663296 | bytes 100663 | tf_op jit(solution)/shard_map/pallas_call | solution.py:51
  13.3 0.1 collective-permute-start.4
  13.4 1.2 %collective-permute-done.4 = f32[2,4,16,128]{3,2,1,0:T(8,128)S(1)} collective-permute-done((f32[2,4,16,128]{3,2,1,0:T(8,128)S(1)}, f32[2,4,16,128]{3,2,1,0:T(8,128)S(1)}, u32[]{:S(2)}, u32[]{:S(2)}) %collective-permute-start.4) | collective-permute-done | bytes 65568 | tf_op jit(solution)/shard_map/ppermute | solution.py:186
  14.7 3.2 %collective-permute-start.7 = (bf16[2,4,16,128]{3,2,1,0:T(8,128)(2,1)S(1)}, bf16[2,4,16,128]{3,2,1,0:T(8,128)(2,1)S(1)}, u32[]{:S(2)}, u32[]{:S(2)}) collective-permute-start(bf16[2,4,16,128]{3,2,1,0:T(8,128)(2,1)S(1)} %fusion.1), channel_id=1, source_target_pairs={{0,24},{8,16},{16,8},{24,0},{1,25},{9,17},{17,9},{25,1},{2,26},{10... | collective-permute-start | bytes 98312 | tf_op jit(solution)/shard_map/ppermute | solution.py:27
  17.8 0.2 collective-permute-start.6
  18.0 1.1 %collective-permute-start.5 = (bf16[2,4,16,128]{3,2,1,0:T(8,128)(2,1)S(1)}, bf16[2,4,16,128]{3,2,1,0:T(8,128)(2,1)S(1)}, u32[]{:S(2)}, u32[]{:S(2)}) collective-permute-start(bf16[2,4,16,128]{3,2,1,0:T(8,128)(2,1)S(1)} %fusion.1), channel_id=1, source_target_pairs={{0,8},{8,0},{16,24},{24,16},{1,9},{9,1},{17,25},{25,17},{2,10},{10... | collective-permute-start | bytes 98312 | tf_op jit(solution)/shard_map/ppermute | solution.py:27
  19.1 1.3 %collective-permute-done.7 = bf16[2,4,16,128]{3,2,1,0:T(8,128)(2,1)S(1)} collective-permute-done((bf16[2,4,16,128]{3,2,1,0:T(8,128)(2,1)S(1)}, bf16[2,4,16,128]{3,2,1,0:T(8,128)(2,1)S(1)}, u32[]{:S(2)}, u32[]{:S(2)}) %collective-permute-start.7) | collective-permute-done | bytes 32800 | tf_op jit(solution)/shard_map/ppermute | solution.py:27
  20.5 2.5 %collective-permute-done.6 = bf16[2,4,16,128]{3,2,1,0:T(8,128)(2,1)S(1)} collective-permute-done((bf16[2,4,16,128]{3,2,1,0:T(8,128)(2,1)S(1)}, bf16[2,4,16,128]{3,2,1,0:T(8,128)(2,1)S(1)}, u32[]{:S(2)}, u32[]{:S(2)}) %collective-permute-start.6) | collective-permute-done | bytes 32800 | tf_op jit(solution)/shard_map/ppermute | solution.py:27
  22.9 0.0 collective-permute-done.5
  23.0 2.5 %collective-permute-start.8 = (bf16[2,2,16,128]{3,2,1,0:T(8,128)(2,1)S(1)}, bf16[2,2,16,128]{3,2,1,0:T(8,128)(2,1)S(1)}, u32[]{:S(2)}, u32[]{:S(2)}) collective-permute-start(bf16[2,2,16,128]{3,2,1,0:T(8,128)(2,1)S(1)} %get-tuple-element.17), channel_id=1, source_target_pairs={{0,3},{1,2},{2,1},{3,0},{4,7},{5,6},{6,5},{7,4},{8,11},{9,10},{10,... | collective-permute-start | bytes 49160 | tf_op jit(solution)/shard_map/ppermute | solution.py:27
  25.5 0.5 %collective-permute-start.9 = (bf16[2,2,16,128]{3,2,1,0:T(8,128)(2,1)S(1)}, bf16[2,2,16,128]{3,2,1,0:T(8,128)(2,1)S(1)}, u32[]{:S(2)}, u32[]{:S(2)}) collective-permute-start(bf16[2,2,16,128]{3,2,1,0:T(8,128)(2,1)S(1)} %get-tuple-element.18), channel_id=1, source_target_pairs={{0,2},{1,3},{2,0},{3,1},{4,6},{5,7},{6,4},{7,5},{8,10},{9,11},{10,... | collective-permute-start | bytes 49160 | tf_op jit(solution)/shard_map/ppermute | solution.py:27
  26.0 0.5 %collective-permute-start.10 = (bf16[2,2,16,128]{3,2,1,0:T(8,128)(2,1)S(1)}, bf16[2,2,16,128]{3,2,1,0:T(8,128)(2,1)S(1)}, u32[]{:S(2)}, u32[]{:S(2)}) collective-permute-start(bf16[2,2,16,128]{3,2,1,0:T(8,128)(2,1)S(1)} %get-tuple-element.19), channel_id=1, source_target_pairs={{0,1},{1,0},{2,3},{3,2},{4,5},{5,4},{6,7},{7,6},{8,9},{9,8},{10,11... | collective-permute-start | bytes 49160 | tf_op jit(solution)/shard_map/ppermute | solution.py:27
  26.6 1.1 %collective-permute-done.8 = bf16[2,2,16,128]{3,2,1,0:T(8,128)(2,1)S(1)} collective-permute-done((bf16[2,2,16,128]{3,2,1,0:T(8,128)(2,1)S(1)}, bf16[2,2,16,128]{3,2,1,0:T(8,128)(2,1)S(1)}, u32[]{:S(2)}, u32[]{:S(2)}) %collective-permute-start.8) | collective-permute-done | bytes 16416 | tf_op jit(solution)/shard_map/ppermute | solution.py:27
  27.7 1.5 %collective-permute-done.9 = bf16[2,2,16,128]{3,2,1,0:T(8,128)(2,1)S(1)} collective-permute-done((bf16[2,2,16,128]{3,2,1,0:T(8,128)(2,1)S(1)}, bf16[2,2,16,128]{3,2,1,0:T(8,128)(2,1)S(1)}, u32[]{:S(2)}, u32[]{:S(2)}) %collective-permute-start.9) | collective-permute-done | bytes 16416 | tf_op jit(solution)/shard_map/ppermute | solution.py:27
  29.2 0.5 %collective-permute-done.10 = bf16[2,2,16,128]{3,2,1,0:T(8,128)(2,1)S(1)} collective-permute-done((bf16[2,2,16,128]{3,2,1,0:T(8,128)(2,1)S(1)}, bf16[2,2,16,128]{3,2,1,0:T(8,128)(2,1)S(1)}, u32[]{:S(2)}, u32[]{:S(2)}) %collective-permute-start.10) | collective-permute-done | bytes 16416 | tf_op jit(solution)/shard_map/ppermute | solution.py:27
  29.8 0.1 collective-permute-start.11
  29.9 1.3 %shard_map.31 = (bf16[1024,2048]{1,0:T(8,128)(2,1)S(1)}, bf16[2048,8]{1,0:T(8,128)(2,1)S(1)}) custom-call(bf16[8,2048]{1,0:T(8,128)(2,1)S(1)} %get-tuple-element.21.row_ref, bf16[8,2048]{1,0:T(8,128)(2,1)S(1)} %get-tuple-element.20.col_ref.own_ref), custom_call_target="tpu_custom_call" | custom-call | flops 33554432 | bytes 4194304 | tf_op jit(solution)/shard_map/pallas_call | solution.py:129
  31.2 0.0 collective-permute-done.11
  31.2 5.9 %shard_map.32 = bf16[2048,4096]{1,0:T(8,128)(2,1)} custom-call(bf16[1024,2048]{1,0:T(8,128)(2,1)S(1)} %get-tuple-element.7.head_ref, bf16[2048,8]{1,0:T(8,128)(2,1)S(1)} %get-tuple-element.8.flipped_ref, bf16[8,2048]{1,0:T(8,128)(2,1)S(1)} %get-tuple-element.20.col_ref.own_ref, bf16[8,2048]{1,0:T(8,128)(2,1)S(1)} %bitcast.39), custom_call_target="tpu_custom_call" | custom-call | flops 100663296 | bytes 16777216 | tf_op jit(solution)/shard_map/pallas_call | solution.py:148
  (9 shorter events, 0.1 us)
Async XLA Ops:
  0.0 12.2 %copy-start = (bf16[384,128]{1,0:T(8,128)(2,1)S(1)}, bf16[384,128]{1,0:T(8,128)(2,1)}, u32[]{:S(2)}) copy-start(bf16[384,128]{1,0:T(8,128)(2,1)} %refs_1_.3) | copy-start | bytes 294916
  0.0 12.2 %collective-permute-start.3 = (bf16[384,128]{1,0:T(8,128)(2,1)}, bf16[384,128]{1,0:T(8,128)(2,1)S(1)}, u32[]{:S(2)}, u32[]{:S(2)}) collective-permute-start(bf16[384,128]{1,0:T(8,128)(2,1)} %refs_1_.3), channel_id=1, source_target_pairs={{0,16},{8,24},{16,0},{24,8},{1,17},{9,25},{17,1},{25,9},{2,18},{10... | collective-permute-start | bytes 294920 | tf_op jit(solution)/shard_map/ppermute | solution.py:27
  4.0 8.8 %collective-permute-start.2 = (bf16[384,128]{1,0:T(8,128)(2,1)}, bf16[384,128]{1,0:T(8,128)(2,1)S(1)}, u32[]{:S(2)}, u32[]{:S(2)}) collective-permute-start(bf16[384,128]{1,0:T(8,128)(2,1)} %refs_1_.3), channel_id=1, source_target_pairs={{0,24},{8,16},{16,8},{24,0},{1,25},{9,17},{17,9},{25,1},{2,26},{10... | collective-permute-start | bytes 294920 | tf_op jit(solution)/shard_map/ppermute | solution.py:27
  5.4 7.5 %collective-permute-start.1 = (bf16[384,128]{1,0:T(8,128)(2,1)}, bf16[384,128]{1,0:T(8,128)(2,1)S(1)}, u32[]{:S(2)}, u32[]{:S(2)}) collective-permute-start(bf16[384,128]{1,0:T(8,128)(2,1)} %refs_1_.3), channel_id=1, source_target_pairs={{0,8},{8,0},{16,24},{24,16},{1,9},{9,1},{17,25},{25,17},{2,10},{10... | collective-permute-start | bytes 294920 | tf_op jit(solution)/shard_map/ppermute | solution.py:27
  9.5 3.1 %collective-permute-start = (bf16[2,4,1,384,128]{4,3,2,1,0:T(8,128)(2,1)S(1)}, bf16[2,4,1,384,128]{4,3,2,1,0:T(8,128)(2,1)S(1)}, u32[]{:S(2)}, u32[]{:S(2)}) collective-permute-start(bf16[2,4,1,384,128]{4,3,2,1,0:T(8,128)(2,1)S(1)} %constant_dynamic-slice_fusion.5), channel_id=1, source_target_pairs={{0,4},{4,0},{1,5},{5,1},{2,6},{6,2},{3,7},{7,3},{8,12},{12,8},{9,1... | collective-permute-start | bytes 2359304 | tf_op jit(solution)/shard_map/ppermute | solution.py:176
  13.3 1.3 %collective-permute-start.4 = (f32[2,4,16,128]{3,2,1,0:T(8,128)S(1)}, f32[2,4,16,128]{3,2,1,0:T(8,128)S(1)}, u32[]{:S(2)}, u32[]{:S(2)}) collective-permute-start(f32[2,4,16,128]{3,2,1,0:T(8,128)S(1)} %dynamic-slice_bitcast_fusion), channel_id=1, source_target_pairs={{0,4},{4,0},{1,5},{5,1},{2,6},{6,2},{3,7},{7,3},{8,12},{12,8},{9,1... | collective-permute-start | bytes 196616 | tf_op jit(solution)/shard_map/ppermute | solution.py:186
  14.7 5.8 %collective-permute-start.7 = (bf16[2,4,16,128]{3,2,1,0:T(8,128)(2,1)S(1)}, bf16[2,4,16,128]{3,2,1,0:T(8,128)(2,1)S(1)}, u32[]{:S(2)}, u32[]{:S(2)}) collective-permute-start(bf16[2,4,16,128]{3,2,1,0:T(8,128)(2,1)S(1)} %fusion.1), channel_id=1, source_target_pairs={{0,24},{8,16},{16,8},{24,0},{1,25},{9,17},{17,9},{25,1},{2,26},{10... | collective-permute-start | bytes 98312 | tf_op jit(solution)/shard_map/ppermute | solution.py:27
  17.8 5.1 %collective-permute-start.6 = (bf16[2,4,16,128]{3,2,1,0:T(8,128)(2,1)S(1)}, bf16[2,4,16,128]{3,2,1,0:T(8,128)(2,1)S(1)}, u32[]{:S(2)}, u32[]{:S(2)}) collective-permute-start(bf16[2,4,16,128]{3,2,1,0:T(8,128)(2,1)S(1)} %fusion.1), channel_id=1, source_target_pairs={{0,16},{8,24},{16,0},{24,8},{1,17},{9,25},{17,1},{25,9},{2,18},{10... | collective-permute-start | bytes 98312 | tf_op jit(solution)/shard_map/ppermute | solution.py:27
  18.0 4.9 %collective-permute-start.5 = (bf16[2,4,16,128]{3,2,1,0:T(8,128)(2,1)S(1)}, bf16[2,4,16,128]{3,2,1,0:T(8,128)(2,1)S(1)}, u32[]{:S(2)}, u32[]{:S(2)}) collective-permute-start(bf16[2,4,16,128]{3,2,1,0:T(8,128)(2,1)S(1)} %fusion.1), channel_id=1, source_target_pairs={{0,8},{8,0},{16,24},{24,16},{1,9},{9,1},{17,25},{25,17},{2,10},{10... | collective-permute-start | bytes 98312 | tf_op jit(solution)/shard_map/ppermute | solution.py:27
  23.0 4.7 %collective-permute-start.8 = (bf16[2,2,16,128]{3,2,1,0:T(8,128)(2,1)S(1)}, bf16[2,2,16,128]{3,2,1,0:T(8,128)(2,1)S(1)}, u32[]{:S(2)}, u32[]{:S(2)}) collective-permute-start(bf16[2,2,16,128]{3,2,1,0:T(8,128)(2,1)S(1)} %get-tuple-element.17), channel_id=1, source_target_pairs={{0,3},{1,2},{2,1},{3,0},{4,7},{5,6},{6,5},{7,4},{8,11},{9,10},{10,... | collective-permute-start | bytes 49160 | tf_op jit(solution)/shard_map/ppermute | solution.py:27
  25.5 3.7 %collective-permute-start.9 = (bf16[2,2,16,128]{3,2,1,0:T(8,128)(2,1)S(1)}, bf16[2,2,16,128]{3,2,1,0:T(8,128)(2,1)S(1)}, u32[]{:S(2)}, u32[]{:S(2)}) collective-permute-start(bf16[2,2,16,128]{3,2,1,0:T(8,128)(2,1)S(1)} %get-tuple-element.18), channel_id=1, source_target_pairs={{0,2},{1,3},{2,0},{3,1},{4,6},{5,7},{6,4},{7,5},{8,10},{9,11},{10,... | collective-permute-start | bytes 49160 | tf_op jit(solution)/shard_map/ppermute | solution.py:27
  26.0 3.7 %collective-permute-start.10 = (bf16[2,2,16,128]{3,2,1,0:T(8,128)(2,1)S(1)}, bf16[2,2,16,128]{3,2,1,0:T(8,128)(2,1)S(1)}, u32[]{:S(2)}, u32[]{:S(2)}) collective-permute-start(bf16[2,2,16,128]{3,2,1,0:T(8,128)(2,1)S(1)} %get-tuple-element.19), channel_id=1, source_target_pairs={{0,1},{1,0},{2,3},{3,2},{4,5},{5,4},{6,7},{7,6},{8,9},{9,8},{10,11... | collective-permute-start | bytes 49160 | tf_op jit(solution)/shard_map/ppermute | solution.py:27
  29.8 1.4 %collective-permute-start.11 = (bf16[8,1,16,128]{3,2,1,0:T(8,128)(2,1)S(1)}, bf16[8,1,16,128]{3,2,1,0:T(8,128)(2,1)S(1)}, u32[]{:S(2)}, u32[]{:S(2)}) collective-permute-start(bf16[8,1,16,128]{3,2,1,0:T(8,128)(2,1)S(1)} %get-tuple-element.9), channel_id=1, source_target_pairs={{0,4},{4,0},{1,5},{5,1},{2,6},{6,2},{3,7},{7,3},{8,12},{12,8},{9,1... | collective-permute-start | bytes 98312 | tf_op jit(solution)/shard_map/ppermute | solution.py:203

commit v6 on v3

--- a/solution.py
+++ b/solution.py
@@ -187,7 +187,7 @@
         lax.dynamic_index_in_dim(partial, 1 - core, 2, keepdims=False), "core", SWAP
     )
     rounded = total.astype(jnp.bfloat16)
-    for s in range(1, nz):
+    for s in (1, *range(nz - 1, 1, -1)):
         total += flip(rounded, "z", s).astype(jnp.float32)
     values = total.astype(jnp.bfloat16)
 

time: 37.1 us -> 36.9 us (level)
  starting transfers between devices: 13.9 us -> 13 us
  waiting for transfers between devices: 10.6 us -> 11.3 us
    ppermute x9, starting transfers between devices: 13.7 us -> 12.8 us  [flip(): return lax.ppermute(array, axis, [(d, d ^ step) for d in range(count)])]
    ppermute x9, waiting for transfers between devices: 9.26 us -> 9.93 us  [flip(): return lax.ppermute(array, axis, [(d, d ^ step) for d in range(count)])]
where the time goes in v6:
time: 36.9 us; the launch traced here: 36.7 us
  starting transfers between devices  13 us (35%)
  waiting for transfers between devices  11.3 us (31%)
  Pallas kernels  8.29 us (22%)
  matrix products  3.77 us (10%)
    ppermute x9, starting transfers between devices, flip(): return lax.ppermute(array, axis, [(d, d ^ step) for d in range(count)])  12.8 us
    ppermute x9, waiting for transfers between devices, flip(): return lax.ppermute(array, axis, [(d, d ^ step) for d in range(count)])  9.93 us
    pallas_call x1, Pallas kernels, rest_product(): pl.pallas_call(functools.partial(rest_kernel, side, rows // BLOCKS), out_...  5.93 us
    dot_general x1, matrix products, body(): jnp.einsum('ri,prk->pki', coeffs, cholesky, preferred_element_type=jnp.fl...  3.77 us
    pallas_call x1, Pallas kernels, head_product(): pl.pallas_call(functools.partial(head_kernel, rows // BLOCKS), out_shape=...  1.31 us
    ppermute x1, waiting for transfers between devices, body(): lax.ppermute(lax.dynamic_index_in_dim(partial, 1 - core, 2, keepdims=Fals...  1.24 us
    pallas_call x3, Pallas kernels, project(): pl.pallas_call(functools.partial(project_kernel, len(lefts), steps), out_...  1.04 us
  transfers between devices with their start and end apart: 12, of which 9 were waited for; matrix products, arithmetic and copies ran while one was open for 10% of the time, Pallas kernels for 6%

profile of v6, /device:TPU:0, one launch (start us, length us, event | category | flops | bytes accessed | tf_op | source)
XLA Modules:
  0.0 36.7 jit_solution(443125265463961630)
XLA Ops:
  0.0 0.0 copy-start
  0.0 5.0 %collective-permute-start.3 = (bf16[384,128]{1,0:T(8,128)(2,1)}, bf16[384,128]{1,0:T(8,128)(2,1)S(1)}, u32[]{:S(2)}, u32[]{:S(2)}) collective-permute-start(bf16[384,128]{1,0:T(8,128)(2,1)} %refs_1_.3), channel_id=1, source_target_pairs={{0,24},{8,16},{16,8},{24,0},{1,25},{9,17},{17,9},{25,1},{2,26},{10... | collective-permute-start | bytes 294920 | tf_op jit(solution)/shard_map/ppermute | solution.py:27
  5.1 0.0 collective-permute-start.2
  5.1 0.6 %collective-permute-start.1 = (bf16[384,128]{1,0:T(8,128)(2,1)}, bf16[384,128]{1,0:T(8,128)(2,1)S(1)}, u32[]{:S(2)}, u32[]{:S(2)}) collective-permute-start(bf16[384,128]{1,0:T(8,128)(2,1)} %refs_1_.3), channel_id=1, source_target_pairs={{0,16},{8,24},{16,0},{24,8},{1,17},{9,25},{17,1},{25,9},{2,18},{10... | collective-permute-start | bytes 294920 | tf_op jit(solution)/shard_map/ppermute | solution.py:27
  5.7 3.8 %convolution_convert_fusion = bf16[2,3072,128]{2,1,0:T(8,128)(2,1)S(1)} fusion(bf16[2,384,3072]{2,1,0:T(8,128)(2,1)} %param.2, bf16[384,128]{1,0:T(8,128)(2,1)} %refs_1_.3), kind=kOutput, calls=%fused_computation | convolution fusion | flops 604766208 | bytes 6389760 | tf_op jit(solution)/shard_map/ri,prk->pki/dot_general | solution.py:173
  9.5 0.1 constant_dynamic-slice_fusion.5
  9.5 0.1 collective-permute-start
  9.6 0.0 collective-permute-done.3.refs_3_
  9.6 1.8 %collective-permute-done.2.refs_2_ = bf16[384,128]{1,0:T(8,128)(2,1)S(1)} collective-permute-done((bf16[384,128]{1,0:T(8,128)(2,1)}, bf16[384,128]{1,0:T(8,128)(2,1)S(1)}, u32[]{:S(2)}, u32[]{:S(2)}) %collective-permute-start.2) | collective-permute-done | bytes 98336 | tf_op jit(solution)/shard_map/ppermute | solution.py:27
  11.4 0.0 copy-done
  11.4 0.4 shard_map.28.refs_4_
  11.8 0.1 collective-permute-done.refs_0_.refs_1_
  11.9 0.4 shard_map.29.refs_3_
  12.2 1.3 %collective-permute-done.1.refs_2_ = bf16[384,128]{1,0:T(8,128)(2,1)S(1)} collective-permute-done((bf16[384,128]{1,0:T(8,128)(2,1)}, bf16[384,128]{1,0:T(8,128)(2,1)S(1)}, u32[]{:S(2)}, u32[]{:S(2)}) %collective-permute-start.1) | collective-permute-done | bytes 98336 | tf_op jit(solution)/shard_map/ppermute | solution.py:27
  13.5 0.3 shard_map.30
  13.9 0.1 collective-permute-start.4
  14.0 1.2 %collective-permute-done.4 = f32[2,4,16,128]{3,2,1,0:T(8,128)S(1)} collective-permute-done((f32[2,4,16,128]{3,2,1,0:T(8,128)S(1)}, f32[2,4,16,128]{3,2,1,0:T(8,128)S(1)}, u32[]{:S(2)}, u32[]{:S(2)}) %collective-permute-start.4) | collective-permute-done | bytes 65568 | tf_op jit(solution)/shard_map/ppermute | solution.py:186
  15.2 1.5 %collective-permute-start.7 = (bf16[2,4,16,128]{3,2,1,0:T(8,128)(2,1)S(1)}, bf16[2,4,16,128]{3,2,1,0:T(8,128)(2,1)S(1)}, u32[]{:S(2)}, u32[]{:S(2)}) collective-permute-start(bf16[2,4,16,128]{3,2,1,0:T(8,128)(2,1)S(1)} %fusion.1), channel_id=1, source_target_pairs={{0,16},{8,24},{16,0},{24,8},{1,17},{9,25},{17,1},{25,9},{2,18},{10... | collective-permute-start | bytes 98312 | tf_op jit(solution)/shard_map/ppermute | solution.py:27
  16.7 1.2 %collective-permute-start.6 = (bf16[2,4,16,128]{3,2,1,0:T(8,128)(2,1)S(1)}, bf16[2,4,16,128]{3,2,1,0:T(8,128)(2,1)S(1)}, u32[]{:S(2)}, u32[]{:S(2)}) collective-permute-start(bf16[2,4,16,128]{3,2,1,0:T(8,128)(2,1)S(1)} %fusion.1), channel_id=1, source_target_pairs={{0,24},{8,16},{16,8},{24,0},{1,25},{9,17},{17,9},{25,1},{2,26},{10... | collective-permute-start | bytes 98312 | tf_op jit(solution)/shard_map/ppermute | solution.py:27
  17.9 0.9 %collective-permute-start.5 = (bf16[2,4,16,128]{3,2,1,0:T(8,128)(2,1)S(1)}, bf16[2,4,16,128]{3,2,1,0:T(8,128)(2,1)S(1)}, u32[]{:S(2)}, u32[]{:S(2)}) collective-permute-start(bf16[2,4,16,128]{3,2,1,0:T(8,128)(2,1)S(1)} %fusion.1), channel_id=1, source_target_pairs={{0,8},{8,0},{16,24},{24,16},{1,9},{9,1},{17,25},{25,17},{2,10},{10... | collective-permute-start | bytes 98312 | tf_op jit(solution)/shard_map/ppermute | solution.py:27
  18.8 1.5 %collective-permute-done.7 = bf16[2,4,16,128]{3,2,1,0:T(8,128)(2,1)S(1)} collective-permute-done((bf16[2,4,16,128]{3,2,1,0:T(8,128)(2,1)S(1)}, bf16[2,4,16,128]{3,2,1,0:T(8,128)(2,1)S(1)}, u32[]{:S(2)}, u32[]{:S(2)}) %collective-permute-start.7) | collective-permute-done | bytes 32800 | tf_op jit(solution)/shard_map/ppermute | solution.py:27
  20.3 2.2 %collective-permute-done.6 = bf16[2,4,16,128]{3,2,1,0:T(8,128)(2,1)S(1)} collective-permute-done((bf16[2,4,16,128]{3,2,1,0:T(8,128)(2,1)S(1)}, bf16[2,4,16,128]{3,2,1,0:T(8,128)(2,1)S(1)}, u32[]{:S(2)}, u32[]{:S(2)}) %collective-permute-start.6) | collective-permute-done | bytes 32800 | tf_op jit(solution)/shard_map/ppermute | solution.py:27
  22.4 0.0 collective-permute-done.5
  22.5 2.5 %collective-permute-start.8 = (bf16[2,2,16,128]{3,2,1,0:T(8,128)(2,1)S(1)}, bf16[2,2,16,128]{3,2,1,0:T(8,128)(2,1)S(1)}, u32[]{:S(2)}, u32[]{:S(2)}) collective-permute-start(bf16[2,2,16,128]{3,2,1,0:T(8,128)(2,1)S(1)} %get-tuple-element.17), channel_id=1, source_target_pairs={{0,3},{1,2},{2,1},{3,0},{4,7},{5,6},{6,5},{7,4},{8,11},{9,10},{10,... | collective-permute-start | bytes 49160 | tf_op jit(solution)/shard_map/ppermute | solution.py:27
  25.0 0.5 %collective-permute-start.9 = (bf16[2,2,16,128]{3,2,1,0:T(8,128)(2,1)S(1)}, bf16[2,2,16,128]{3,2,1,0:T(8,128)(2,1)S(1)}, u32[]{:S(2)}, u32[]{:S(2)}) collective-permute-start(bf16[2,2,16,128]{3,2,1,0:T(8,128)(2,1)S(1)} %get-tuple-element.18), channel_id=1, source_target_pairs={{0,2},{1,3},{2,0},{3,1},{4,6},{5,7},{6,4},{7,5},{8,10},{9,11},{10,... | collective-permute-start | bytes 49160 | tf_op jit(solution)/shard_map/ppermute | solution.py:27
  25.5 0.5 %collective-permute-start.10 = (bf16[2,2,16,128]{3,2,1,0:T(8,128)(2,1)S(1)}, bf16[2,2,16,128]{3,2,1,0:T(8,128)(2,1)S(1)}, u32[]{:S(2)}, u32[]{:S(2)}) collective-permute-start(bf16[2,2,16,128]{3,2,1,0:T(8,128)(2,1)S(1)} %get-tuple-element.19), channel_id=1, source_target_pairs={{0,1},{1,0},{2,3},{3,2},{4,5},{5,4},{6,7},{7,6},{8,9},{9,8},{10,11... | collective-permute-start | bytes 49160 | tf_op jit(solution)/shard_map/ppermute | solution.py:27
  26.0 1.1 %collective-permute-done.8 = bf16[2,2,16,128]{3,2,1,0:T(8,128)(2,1)S(1)} collective-permute-done((bf16[2,2,16,128]{3,2,1,0:T(8,128)(2,1)S(1)}, bf16[2,2,16,128]{3,2,1,0:T(8,128)(2,1)S(1)}, u32[]{:S(2)}, u32[]{:S(2)}) %collective-permute-start.8) | collective-permute-done | bytes 16416 | tf_op jit(solution)/shard_map/ppermute | solution.py:27
  27.2 1.5 %collective-permute-done.9 = bf16[2,2,16,128]{3,2,1,0:T(8,128)(2,1)S(1)} collective-permute-done((bf16[2,2,16,128]{3,2,1,0:T(8,128)(2,1)S(1)}, bf16[2,2,16,128]{3,2,1,0:T(8,128)(2,1)S(1)}, u32[]{:S(2)}, u32[]{:S(2)}) %collective-permute-start.9) | collective-permute-done | bytes 16416 | tf_op jit(solution)/shard_map/ppermute | solution.py:27
  28.7 0.5 %collective-permute-done.10 = bf16[2,2,16,128]{3,2,1,0:T(8,128)(2,1)S(1)} collective-permute-done((bf16[2,2,16,128]{3,2,1,0:T(8,128)(2,1)S(1)}, bf16[2,2,16,128]{3,2,1,0:T(8,128)(2,1)S(1)}, u32[]{:S(2)}, u32[]{:S(2)}) %collective-permute-start.10) | collective-permute-done | bytes 16416 | tf_op jit(solution)/shard_map/ppermute | solution.py:27
  29.3 0.1 collective-permute-start.11
  29.4 1.3 %shard_map.31 = (bf16[1024,2048]{1,0:T(8,128)(2,1)S(1)}, bf16[2048,8]{1,0:T(8,128)(2,1)S(1)}) custom-call(bf16[8,2048]{1,0:T(8,128)(2,1)S(1)} %get-tuple-element.21.row_ref, bf16[8,2048]{1,0:T(8,128)(2,1)S(1)} %get-tuple-element.20.col_ref.own_ref), custom_call_target="tpu_custom_call" | custom-call | flops 33554432 | bytes 4194304 | tf_op jit(solution)/shard_map/pallas_call | solution.py:129
  30.7 0.0 collective-permute-done.11
  30.7 5.9 %shard_map.32 = bf16[2048,4096]{1,0:T(8,128)(2,1)} custom-call(bf16[1024,2048]{1,0:T(8,128)(2,1)S(1)} %get-tuple-element.7.head_ref, bf16[2048,8]{1,0:T(8,128)(2,1)S(1)} %get-tuple-element.8.flipped_ref, bf16[8,2048]{1,0:T(8,128)(2,1)S(1)} %get-tuple-element.20.col_ref.own_ref, bf16[8,2048]{1,0:T(8,128)(2,1)S(1)} %bitcast.39), custom_call_target="tpu_custom_call" | custom-call | flops 100663296 | bytes 16777216 | tf_op jit(solution)/shard_map/pallas_call | solution.py:148
  (9 shorter events, 0.1 us)
Async XLA Ops:
  0.0 11.4 %copy-start = (bf16[384,128]{1,0:T(8,128)(2,1)S(1)}, bf16[384,128]{1,0:T(8,128)(2,1)}, u32[]{:S(2)}) copy-start(bf16[384,128]{1,0:T(8,128)(2,1)} %refs_1_.3) | copy-start | bytes 294916
  0.0 9.6 %collective-permute-start.3 = (bf16[384,128]{1,0:T(8,128)(2,1)}, bf16[384,128]{1,0:T(8,128)(2,1)S(1)}, u32[]{:S(2)}, u32[]{:S(2)}) collective-permute-start(bf16[384,128]{1,0:T(8,128)(2,1)} %refs_1_.3), channel_id=1, source_target_pairs={{0,24},{8,16},{16,8},{24,0},{1,25},{9,17},{17,9},{25,1},{2,26},{10... | collective-permute-start | bytes 294920 | tf_op jit(solution)/shard_map/ppermute | solution.py:27
  5.1 6.4 %collective-permute-start.2 = (bf16[384,128]{1,0:T(8,128)(2,1)}, bf16[384,128]{1,0:T(8,128)(2,1)S(1)}, u32[]{:S(2)}, u32[]{:S(2)}) collective-permute-start(bf16[384,128]{1,0:T(8,128)(2,1)} %refs_1_.3), channel_id=1, source_target_pairs={{0,8},{8,0},{16,24},{24,16},{1,9},{9,1},{17,25},{25,17},{2,10},{10... | collective-permute-start | bytes 294920 | tf_op jit(solution)/shard_map/ppermute | solution.py:27
  5.1 8.5 %collective-permute-start.1 = (bf16[384,128]{1,0:T(8,128)(2,1)}, bf16[384,128]{1,0:T(8,128)(2,1)S(1)}, u32[]{:S(2)}, u32[]{:S(2)}) collective-permute-start(bf16[384,128]{1,0:T(8,128)(2,1)} %refs_1_.3), channel_id=1, source_target_pairs={{0,16},{8,24},{16,0},{24,8},{1,17},{9,25},{17,1},{25,9},{2,18},{10... | collective-permute-start | bytes 294920 | tf_op jit(solution)/shard_map/ppermute | solution.py:27
  9.5 2.4 %collective-permute-start = (bf16[2,4,1,384,128]{4,3,2,1,0:T(8,128)(2,1)S(1)}, bf16[2,4,1,384,128]{4,3,2,1,0:T(8,128)(2,1)S(1)}, u32[]{:S(2)}, u32[]{:S(2)}) collective-permute-start(bf16[2,4,1,384,128]{4,3,2,1,0:T(8,128)(2,1)S(1)} %constant_dynamic-slice_fusion.5), channel_id=1, source_target_pairs={{0,4},{4,0},{1,5},{5,1},{2,6},{6,2},{3,7},{7,3},{8,12},{12,8},{9,1... | collective-permute-start | bytes 2359304 | tf_op jit(solution)/shard_map/ppermute | solution.py:176
  13.9 1.3 %collective-permute-start.4 = (f32[2,4,16,128]{3,2,1,0:T(8,128)S(1)}, f32[2,4,16,128]{3,2,1,0:T(8,128)S(1)}, u32[]{:S(2)}, u32[]{:S(2)}) collective-permute-start(f32[2,4,16,128]{3,2,1,0:T(8,128)S(1)} %dynamic-slice_bitcast_fusion), channel_id=1, source_target_pairs={{0,4},{4,0},{1,5},{5,1},{2,6},{6,2},{3,7},{7,3},{8,12},{12,8},{9,1... | collective-permute-start | bytes 196616 | tf_op jit(solution)/shard_map/ppermute | solution.py:186
  15.2 5.0 %collective-permute-start.7 = (bf16[2,4,16,128]{3,2,1,0:T(8,128)(2,1)S(1)}, bf16[2,4,16,128]{3,2,1,0:T(8,128)(2,1)S(1)}, u32[]{:S(2)}, u32[]{:S(2)}) collective-permute-start(bf16[2,4,16,128]{3,2,1,0:T(8,128)(2,1)S(1)} %fusion.1), channel_id=1, source_target_pairs={{0,16},{8,24},{16,0},{24,8},{1,17},{9,25},{17,1},{25,9},{2,18},{10... | collective-permute-start | bytes 98312 | tf_op jit(solution)/shard_map/ppermute | solution.py:27
  16.7 5.7 %collective-permute-start.6 = (bf16[2,4,16,128]{3,2,1,0:T(8,128)(2,1)S(1)}, bf16[2,4,16,128]{3,2,1,0:T(8,128)(2,1)S(1)}, u32[]{:S(2)}, u32[]{:S(2)}) collective-permute-start(bf16[2,4,16,128]{3,2,1,0:T(8,128)(2,1)S(1)} %fusion.1), channel_id=1, source_target_pairs={{0,24},{8,16},{16,8},{24,0},{1,25},{9,17},{17,9},{25,1},{2,26},{10... | collective-permute-start | bytes 98312 | tf_op jit(solution)/shard_map/ppermute | solution.py:27
  17.9 4.5 %collective-permute-start.5 = (bf16[2,4,16,128]{3,2,1,0:T(8,128)(2,1)S(1)}, bf16[2,4,16,128]{3,2,1,0:T(8,128)(2,1)S(1)}, u32[]{:S(2)}, u32[]{:S(2)}) collective-permute-start(bf16[2,4,16,128]{3,2,1,0:T(8,128)(2,1)S(1)} %fusion.1), channel_id=1, source_target_pairs={{0,8},{8,0},{16,24},{24,16},{1,9},{9,1},{17,25},{25,17},{2,10},{10... | collective-permute-start | bytes 98312 | tf_op jit(solution)/shard_map/ppermute | solution.py:27
  22.5 4.7 %collective-permute-start.8 = (bf16[2,2,16,128]{3,2,1,0:T(8,128)(2,1)S(1)}, bf16[2,2,16,128]{3,2,1,0:T(8,128)(2,1)S(1)}, u32[]{:S(2)}, u32[]{:S(2)}) collective-permute-start(bf16[2,2,16,128]{3,2,1,0:T(8,128)(2,1)S(1)} %get-tuple-element.17), channel_id=1, source_target_pairs={{0,3},{1,2},{2,1},{3,0},{4,7},{5,6},{6,5},{7,4},{8,11},{9,10},{10,... | collective-permute-start | bytes 49160 | tf_op jit(solution)/shard_map/ppermute | solution.py:27
  25.0 3.7 %collective-permute-start.9 = (bf16[2,2,16,128]{3,2,1,0:T(8,128)(2,1)S(1)}, bf16[2,2,16,128]{3,2,1,0:T(8,128)(2,1)S(1)}, u32[]{:S(2)}, u32[]{:S(2)}) collective-permute-start(bf16[2,2,16,128]{3,2,1,0:T(8,128)(2,1)S(1)} %get-tuple-element.18), channel_id=1, source_target_pairs={{0,2},{1,3},{2,0},{3,1},{4,6},{5,7},{6,4},{7,5},{8,10},{9,11},{10,... | collective-permute-start | bytes 49160 | tf_op jit(solution)/shard_map/ppermute | solution.py:27
  25.5 3.7 %collective-permute-start.10 = (bf16[2,2,16,128]{3,2,1,0:T(8,128)(2,1)S(1)}, bf16[2,2,16,128]{3,2,1,0:T(8,128)(2,1)S(1)}, u32[]{:S(2)}, u32[]{:S(2)}) collective-permute-start(bf16[2,2,16,128]{3,2,1,0:T(8,128)(2,1)S(1)} %get-tuple-element.19), channel_id=1, source_target_pairs={{0,1},{1,0},{2,3},{3,2},{4,5},{5,4},{6,7},{7,6},{8,9},{9,8},{10,11... | collective-permute-start | bytes 49160 | tf_op jit(solution)/shard_map/ppermute | solution.py:27
  29.3 1.4 %collective-permute-start.11 = (bf16[8,1,16,128]{3,2,1,0:T(8,128)(2,1)S(1)}, bf16[8,1,16,128]{3,2,1,0:T(8,128)(2,1)S(1)}, u32[]{:S(2)}, u32[]{:S(2)}) collective-permute-start(bf16[8,1,16,128]{3,2,1,0:T(8,128)(2,1)S(1)} %get-tuple-element.9), channel_id=1, source_target_pairs={{0,4},{4,0},{1,5},{5,1},{2,6},{6,2},{3,7},{7,3},{8,12},{12,8},{9,1... | collective-permute-start | bytes 98312 | tf_op jit(solution)/shard_map/ppermute | solution.py:203

commit v7 on v6

--- a/solution.py
+++ b/solution.py
@@ -194,7 +194,7 @@
     wide = nz // n_chol
     row_out = pick(values, z, 1, 1)
     seen = [jnp.concatenate([row_out, pick(values, chol, wide, 1)], 1)]
-    for s in range(n_chol - 1, 0, -1):
+    for s in (n_chol - 1, *range(1, n_chol - 1)):
         seen.append(flip(jnp.concatenate([row_out, pick(values, chol ^ s, wide, 1)], 1), "chol", s))
     seen = row_major(jnp.concatenate(seen, 0))
     vecs = seen.shape[0]

time: 36.9 us -> 36.9 us (level)
  no operation moved by 1% of the time
where the time goes in v7:
time: 36.9 us; the launch traced here: 36.7 us
  starting transfers between devices  13 us (35%)
  waiting for transfers between devices  11.3 us (31%)
  Pallas kernels  8.29 us (22%)
  matrix products  3.77 us (10%)
    ppermute x9, starting transfers between devices, flip(): return lax.ppermute(array, axis, [(d, d ^ step) for d in range(count)])  12.8 us
    ppermute x9, waiting for transfers between devices, flip(): return lax.ppermute(array, axis, [(d, d ^ step) for d in range(count)])  9.96 us
    pallas_call x1, Pallas kernels, rest_product(): pl.pallas_call(functools.partial(rest_kernel, side, rows // BLOCKS), out_...  5.93 us
    dot_general x1, matrix products, body(): jnp.einsum('ri,prk->pki', coeffs, cholesky, preferred_element_type=jnp.fl...  3.77 us
    pallas_call x1, Pallas kernels, head_product(): pl.pallas_call(functools.partial(head_kernel, rows // BLOCKS), out_shape=...  1.31 us
    ppermute x1, waiting for transfers between devices, body(): lax.ppermute(lax.dynamic_index_in_dim(partial, 1 - core, 2, keepdims=Fals...  1.24 us
    pallas_call x3, Pallas kernels, project(): pl.pallas_call(functools.partial(project_kernel, len(lefts), steps), out_...  1.04 us
  transfers between devices with their start and end apart: 12, of which 9 were waited for; matrix products, arithmetic and copies ran while one was open for 10% of the time, Pallas kernels for 6%

profile of v7, /device:TPU:0, one launch (start us, length us, event | category | flops | bytes accessed | tf_op | source)
XLA Modules:
  0.0 36.7 jit_solution(8707963552441703456)
XLA Ops:
  0.0 0.0 copy-start
  0.0 5.0 %collective-permute-start.3 = (bf16[384,128]{1,0:T(8,128)(2,1)}, bf16[384,128]{1,0:T(8,128)(2,1)S(1)}, u32[]{:S(2)}, u32[]{:S(2)}) collective-permute-start(bf16[384,128]{1,0:T(8,128)(2,1)} %refs_1_.3), channel_id=1, source_target_pairs={{0,24},{8,16},{16,8},{24,0},{1,25},{9,17},{17,9},{25,1},{2,26},{10... | collective-permute-start | bytes 294920 | tf_op jit(solution)/shard_map/ppermute | solution.py:27
  5.1 0.0 collective-permute-start.2
  5.1 0.6 %collective-permute-start.1 = (bf16[384,128]{1,0:T(8,128)(2,1)}, bf16[384,128]{1,0:T(8,128)(2,1)S(1)}, u32[]{:S(2)}, u32[]{:S(2)}) collective-permute-start(bf16[384,128]{1,0:T(8,128)(2,1)} %refs_1_.3), channel_id=1, source_target_pairs={{0,16},{8,24},{16,0},{24,8},{1,17},{9,25},{17,1},{25,9},{2,18},{10... | collective-permute-start | bytes 294920 | tf_op jit(solution)/shard_map/ppermute | solution.py:27
  5.7 3.8 %convolution_convert_fusion = bf16[2,3072,128]{2,1,0:T(8,128)(2,1)S(1)} fusion(bf16[2,384,3072]{2,1,0:T(8,128)(2,1)} %param.2, bf16[384,128]{1,0:T(8,128)(2,1)} %refs_1_.3), kind=kOutput, calls=%fused_computation | convolution fusion | flops 604766208 | bytes 6389760 | tf_op jit(solution)/shard_map/ri,prk->pki/dot_general | solution.py:173
  9.5 0.1 constant_dynamic-slice_fusion.5
  9.5 0.1 collective-permute-start
  9.6 0.0 collective-permute-done.3.refs_3_
  9.6 1.8 %collective-permute-done.2.refs_2_ = bf16[384,128]{1,0:T(8,128)(2,1)S(1)} collective-permute-done((bf16[384,128]{1,0:T(8,128)(2,1)}, bf16[384,128]{1,0:T(8,128)(2,1)S(1)}, u32[]{:S(2)}, u32[]{:S(2)}) %collective-permute-start.2) | collective-permute-done | bytes 98336 | tf_op jit(solution)/shard_map/ppermute | solution.py:27
  11.4 0.0 copy-done
  11.4 0.4 shard_map.28.refs_4_
  11.8 0.1 collective-permute-done.refs_0_.refs_1_
  11.9 0.4 shard_map.29.refs_3_
  12.2 1.3 %collective-permute-done.1.refs_2_ = bf16[384,128]{1,0:T(8,128)(2,1)S(1)} collective-permute-done((bf16[384,128]{1,0:T(8,128)(2,1)}, bf16[384,128]{1,0:T(8,128)(2,1)S(1)}, u32[]{:S(2)}, u32[]{:S(2)}) %collective-permute-start.1) | collective-permute-done | bytes 98336 | tf_op jit(solution)/shard_map/ppermute | solution.py:27
  13.5 0.3 shard_map.30
  13.9 0.1 collective-permute-start.4
  14.0 1.2 %collective-permute-done.4 = f32[2,4,16,128]{3,2,1,0:T(8,128)S(1)} collective-permute-done((f32[2,4,16,128]{3,2,1,0:T(8,128)S(1)}, f32[2,4,16,128]{3,2,1,0:T(8,128)S(1)}, u32[]{:S(2)}, u32[]{:S(2)}) %collective-permute-start.4) | collective-permute-done | bytes 65568 | tf_op jit(solution)/shard_map/ppermute | solution.py:186
  15.2 1.5 %collective-permute-start.7 = (bf16[2,4,16,128]{3,2,1,0:T(8,128)(2,1)S(1)}, bf16[2,4,16,128]{3,2,1,0:T(8,128)(2,1)S(1)}, u32[]{:S(2)}, u32[]{:S(2)}) collective-permute-start(bf16[2,4,16,128]{3,2,1,0:T(8,128)(2,1)S(1)} %fusion.1), channel_id=1, source_target_pairs={{0,16},{8,24},{16,0},{24,8},{1,17},{9,25},{17,1},{25,9},{2,18},{10... | collective-permute-start | bytes 98312 | tf_op jit(solution)/shard_map/ppermute | solution.py:27
  16.7 1.2 %collective-permute-start.6 = (bf16[2,4,16,128]{3,2,1,0:T(8,128)(2,1)S(1)}, bf16[2,4,16,128]{3,2,1,0:T(8,128)(2,1)S(1)}, u32[]{:S(2)}, u32[]{:S(2)}) collective-permute-start(bf16[2,4,16,128]{3,2,1,0:T(8,128)(2,1)S(1)} %fusion.1), channel_id=1, source_target_pairs={{0,24},{8,16},{16,8},{24,0},{1,25},{9,17},{17,9},{25,1},{2,26},{10... | collective-permute-start | bytes 98312 | tf_op jit(solution)/shard_map/ppermute | solution.py:27
  17.9 0.9 %collective-permute-start.5 = (bf16[2,4,16,128]{3,2,1,0:T(8,128)(2,1)S(1)}, bf16[2,4,16,128]{3,2,1,0:T(8,128)(2,1)S(1)}, u32[]{:S(2)}, u32[]{:S(2)}) collective-permute-start(bf16[2,4,16,128]{3,2,1,0:T(8,128)(2,1)S(1)} %fusion.1), channel_id=1, source_target_pairs={{0,8},{8,0},{16,24},{24,16},{1,9},{9,1},{17,25},{25,17},{2,10},{10... | collective-permute-start | bytes 98312 | tf_op jit(solution)/shard_map/ppermute | solution.py:27
  18.8 1.5 %collective-permute-done.7 = bf16[2,4,16,128]{3,2,1,0:T(8,128)(2,1)S(1)} collective-permute-done((bf16[2,4,16,128]{3,2,1,0:T(8,128)(2,1)S(1)}, bf16[2,4,16,128]{3,2,1,0:T(8,128)(2,1)S(1)}, u32[]{:S(2)}, u32[]{:S(2)}) %collective-permute-start.7) | collective-permute-done | bytes 32800 | tf_op jit(solution)/shard_map/ppermute | solution.py:27
  20.3 2.2 %collective-permute-done.6 = bf16[2,4,16,128]{3,2,1,0:T(8,128)(2,1)S(1)} collective-permute-done((bf16[2,4,16,128]{3,2,1,0:T(8,128)(2,1)S(1)}, bf16[2,4,16,128]{3,2,1,0:T(8,128)(2,1)S(1)}, u32[]{:S(2)}, u32[]{:S(2)}) %collective-permute-start.6) | collective-permute-done | bytes 32800 | tf_op jit(solution)/shard_map/ppermute | solution.py:27
  22.4 0.0 collective-permute-done.5
  22.5 2.5 %collective-permute-start.8 = (bf16[2,2,16,128]{3,2,1,0:T(8,128)(2,1)S(1)}, bf16[2,2,16,128]{3,2,1,0:T(8,128)(2,1)S(1)}, u32[]{:S(2)}, u32[]{:S(2)}) collective-permute-start(bf16[2,2,16,128]{3,2,1,0:T(8,128)(2,1)S(1)} %get-tuple-element.17), channel_id=1, source_target_pairs={{0,3},{1,2},{2,1},{3,0},{4,7},{5,6},{6,5},{7,4},{8,11},{9,10},{10,... | collective-permute-start | bytes 49160 | tf_op jit(solution)/shard_map/ppermute | solution.py:27
  25.0 0.5 %collective-permute-start.9 = (bf16[2,2,16,128]{3,2,1,0:T(8,128)(2,1)S(1)}, bf16[2,2,16,128]{3,2,1,0:T(8,128)(2,1)S(1)}, u32[]{:S(2)}, u32[]{:S(2)}) collective-permute-start(bf16[2,2,16,128]{3,2,1,0:T(8,128)(2,1)S(1)} %get-tuple-element.18), channel_id=1, source_target_pairs={{0,1},{1,0},{2,3},{3,2},{4,5},{5,4},{6,7},{7,6},{8,9},{9,8},{10,11... | collective-permute-start | bytes 49160 | tf_op jit(solution)/shard_map/ppermute | solution.py:27
  25.5 0.5 %collective-permute-start.10 = (bf16[2,2,16,128]{3,2,1,0:T(8,128)(2,1)S(1)}, bf16[2,2,16,128]{3,2,1,0:T(8,128)(2,1)S(1)}, u32[]{:S(2)}, u32[]{:S(2)}) collective-permute-start(bf16[2,2,16,128]{3,2,1,0:T(8,128)(2,1)S(1)} %get-tuple-element.19), channel_id=1, source_target_pairs={{0,2},{1,3},{2,0},{3,1},{4,6},{5,7},{6,4},{7,5},{8,10},{9,11},{10,... | collective-permute-start | bytes 49160 | tf_op jit(solution)/shard_map/ppermute | solution.py:27
  26.0 1.1 %collective-permute-done.8 = bf16[2,2,16,128]{3,2,1,0:T(8,128)(2,1)S(1)} collective-permute-done((bf16[2,2,16,128]{3,2,1,0:T(8,128)(2,1)S(1)}, bf16[2,2,16,128]{3,2,1,0:T(8,128)(2,1)S(1)}, u32[]{:S(2)}, u32[]{:S(2)}) %collective-permute-start.8) | collective-permute-done | bytes 16416 | tf_op jit(solution)/shard_map/ppermute | solution.py:27
  27.2 1.5 %collective-permute-done.9 = bf16[2,2,16,128]{3,2,1,0:T(8,128)(2,1)S(1)} collective-permute-done((bf16[2,2,16,128]{3,2,1,0:T(8,128)(2,1)S(1)}, bf16[2,2,16,128]{3,2,1,0:T(8,128)(2,1)S(1)}, u32[]{:S(2)}, u32[]{:S(2)}) %collective-permute-start.9) | collective-permute-done | bytes 16416 | tf_op jit(solution)/shard_map/ppermute | solution.py:27
  28.7 0.5 %collective-permute-done.10 = bf16[2,2,16,128]{3,2,1,0:T(8,128)(2,1)S(1)} collective-permute-done((bf16[2,2,16,128]{3,2,1,0:T(8,128)(2,1)S(1)}, bf16[2,2,16,128]{3,2,1,0:T(8,128)(2,1)S(1)}, u32[]{:S(2)}, u32[]{:S(2)}) %collective-permute-start.10) | collective-permute-done | bytes 16416 | tf_op jit(solution)/shard_map/ppermute | solution.py:27
  29.3 0.1 collective-permute-start.11
  29.4 1.3 %shard_map.31 = (bf16[1024,2048]{1,0:T(8,128)(2,1)S(1)}, bf16[2048,8]{1,0:T(8,128)(2,1)S(1)}) custom-call(bf16[8,2048]{1,0:T(8,128)(2,1)S(1)} %get-tuple-element.21.row_ref, bf16[8,2048]{1,0:T(8,128)(2,1)S(1)} %get-tuple-element.20.col_ref.own_ref), custom_call_target="tpu_custom_call" | custom-call | flops 33554432 | bytes 4194304 | tf_op jit(solution)/shard_map/pallas_call | solution.py:129
  30.7 0.0 collective-permute-done.11
  30.8 5.9 %shard_map.32 = bf16[2048,4096]{1,0:T(8,128)(2,1)} custom-call(bf16[1024,2048]{1,0:T(8,128)(2,1)S(1)} %get-tuple-element.7.head_ref, bf16[2048,8]{1,0:T(8,128)(2,1)S(1)} %get-tuple-element.8.flipped_ref, bf16[8,2048]{1,0:T(8,128)(2,1)S(1)} %get-tuple-element.20.col_ref.own_ref, bf16[8,2048]{1,0:T(8,128)(2,1)S(1)} %bitcast.39), custom_call_target="tpu_custom_call" | custom-call | flops 100663296 | bytes 16777216 | tf_op jit(solution)/shard_map/pallas_call | solution.py:148
  (9 shorter events, 0.1 us)
Async XLA Ops:
  0.0 11.4 %copy-start = (bf16[384,128]{1,0:T(8,128)(2,1)S(1)}, bf16[384,128]{1,0:T(8,128)(2,1)}, u32[]{:S(2)}) copy-start(bf16[384,128]{1,0:T(8,128)(2,1)} %refs_1_.3) | copy-start | bytes 294916
  0.0 9.6 %collective-permute-start.3 = (bf16[384,128]{1,0:T(8,128)(2,1)}, bf16[384,128]{1,0:T(8,128)(2,1)S(1)}, u32[]{:S(2)}, u32[]{:S(2)}) collective-permute-start(bf16[384,128]{1,0:T(8,128)(2,1)} %refs_1_.3), channel_id=1, source_target_pairs={{0,24},{8,16},{16,8},{24,0},{1,25},{9,17},{17,9},{25,1},{2,26},{10... | collective-permute-start | bytes 294920 | tf_op jit(solution)/shard_map/ppermute | solution.py:27
  5.1 6.4 %collective-permute-start.2 = (bf16[384,128]{1,0:T(8,128)(2,1)}, bf16[384,128]{1,0:T(8,128)(2,1)S(1)}, u32[]{:S(2)}, u32[]{:S(2)}) collective-permute-start(bf16[384,128]{1,0:T(8,128)(2,1)} %refs_1_.3), channel_id=1, source_target_pairs={{0,8},{8,0},{16,24},{24,16},{1,9},{9,1},{17,25},{25,17},{2,10},{10... | collective-permute-start | bytes 294920 | tf_op jit(solution)/shard_map/ppermute | solution.py:27
  5.1 8.5 %collective-permute-start.1 = (bf16[384,128]{1,0:T(8,128)(2,1)}, bf16[384,128]{1,0:T(8,128)(2,1)S(1)}, u32[]{:S(2)}, u32[]{:S(2)}) collective-permute-start(bf16[384,128]{1,0:T(8,128)(2,1)} %refs_1_.3), channel_id=1, source_target_pairs={{0,16},{8,24},{16,0},{24,8},{1,17},{9,25},{17,1},{25,9},{2,18},{10... | collective-permute-start | bytes 294920 | tf_op jit(solution)/shard_map/ppermute | solution.py:27
  9.5 2.4 %collective-permute-start = (bf16[2,4,1,384,128]{4,3,2,1,0:T(8,128)(2,1)S(1)}, bf16[2,4,1,384,128]{4,3,2,1,0:T(8,128)(2,1)S(1)}, u32[]{:S(2)}, u32[]{:S(2)}) collective-permute-start(bf16[2,4,1,384,128]{4,3,2,1,0:T(8,128)(2,1)S(1)} %constant_dynamic-slice_fusion.5), channel_id=1, source_target_pairs={{0,4},{4,0},{1,5},{5,1},{2,6},{6,2},{3,7},{7,3},{8,12},{12,8},{9,1... | collective-permute-start | bytes 2359304 | tf_op jit(solution)/shard_map/ppermute | solution.py:176
  13.9 1.3 %collective-permute-start.4 = (f32[2,4,16,128]{3,2,1,0:T(8,128)S(1)}, f32[2,4,16,128]{3,2,1,0:T(8,128)S(1)}, u32[]{:S(2)}, u32[]{:S(2)}) collective-permute-start(f32[2,4,16,128]{3,2,1,0:T(8,128)S(1)} %dynamic-slice_bitcast_fusion), channel_id=1, source_target_pairs={{0,4},{4,0},{1,5},{5,1},{2,6},{6,2},{3,7},{7,3},{8,12},{12,8},{9,1... | collective-permute-start | bytes 196616 | tf_op jit(solution)/shard_map/ppermute | solution.py:186
  15.2 5.0 %collective-permute-start.7 = (bf16[2,4,16,128]{3,2,1,0:T(8,128)(2,1)S(1)}, bf16[2,4,16,128]{3,2,1,0:T(8,128)(2,1)S(1)}, u32[]{:S(2)}, u32[]{:S(2)}) collective-permute-start(bf16[2,4,16,128]{3,2,1,0:T(8,128)(2,1)S(1)} %fusion.1), channel_id=1, source_target_pairs={{0,16},{8,24},{16,0},{24,8},{1,17},{9,25},{17,1},{25,9},{2,18},{10... | collective-permute-start | bytes 98312 | tf_op jit(solution)/shard_map/ppermute | solution.py:27
  16.7 5.7 %collective-permute-start.6 = (bf16[2,4,16,128]{3,2,1,0:T(8,128)(2,1)S(1)}, bf16[2,4,16,128]{3,2,1,0:T(8,128)(2,1)S(1)}, u32[]{:S(2)}, u32[]{:S(2)}) collective-permute-start(bf16[2,4,16,128]{3,2,1,0:T(8,128)(2,1)S(1)} %fusion.1), channel_id=1, source_target_pairs={{0,24},{8,16},{16,8},{24,0},{1,25},{9,17},{17,9},{25,1},{2,26},{10... | collective-permute-start | bytes 98312 | tf_op jit(solution)/shard_map/ppermute | solution.py:27
  17.9 4.5 %collective-permute-start.5 = (bf16[2,4,16,128]{3,2,1,0:T(8,128)(2,1)S(1)}, bf16[2,4,16,128]{3,2,1,0:T(8,128)(2,1)S(1)}, u32[]{:S(2)}, u32[]{:S(2)}) collective-permute-start(bf16[2,4,16,128]{3,2,1,0:T(8,128)(2,1)S(1)} %fusion.1), channel_id=1, source_target_pairs={{0,8},{8,0},{16,24},{24,16},{1,9},{9,1},{17,25},{25,17},{2,10},{10... | collective-permute-start | bytes 98312 | tf_op jit(solution)/shard_map/ppermute | solution.py:27
  22.5 4.7 %collective-permute-start.8 = (bf16[2,2,16,128]{3,2,1,0:T(8,128)(2,1)S(1)}, bf16[2,2,16,128]{3,2,1,0:T(8,128)(2,1)S(1)}, u32[]{:S(2)}, u32[]{:S(2)}) collective-permute-start(bf16[2,2,16,128]{3,2,1,0:T(8,128)(2,1)S(1)} %get-tuple-element.17), channel_id=1, source_target_pairs={{0,3},{1,2},{2,1},{3,0},{4,7},{5,6},{6,5},{7,4},{8,11},{9,10},{10,... | collective-permute-start | bytes 49160 | tf_op jit(solution)/shard_map/ppermute | solution.py:27
  25.0 3.7 %collective-permute-start.9 = (bf16[2,2,16,128]{3,2,1,0:T(8,128)(2,1)S(1)}, bf16[2,2,16,128]{3,2,1,0:T(8,128)(2,1)S(1)}, u32[]{:S(2)}, u32[]{:S(2)}) collective-permute-start(bf16[2,2,16,128]{3,2,1,0:T(8,128)(2,1)S(1)} %get-tuple-element.18), channel_id=1, source_target_pairs={{0,1},{1,0},{2,3},{3,2},{4,5},{5,4},{6,7},{7,6},{8,9},{9,8},{10,11... | collective-permute-start | bytes 49160 | tf_op jit(solution)/shard_map/ppermute | solution.py:27
  25.5 3.7 %collective-permute-start.10 = (bf16[2,2,16,128]{3,2,1,0:T(8,128)(2,1)S(1)}, bf16[2,2,16,128]{3,2,1,0:T(8,128)(2,1)S(1)}, u32[]{:S(2)}, u32[]{:S(2)}) collective-permute-start(bf16[2,2,16,128]{3,2,1,0:T(8,128)(2,1)S(1)} %get-tuple-element.19), channel_id=1, source_target_pairs={{0,2},{1,3},{2,0},{3,1},{4,6},{5,7},{6,4},{7,5},{8,10},{9,11},{10,... | collective-permute-start | bytes 49160 | tf_op jit(solution)/shard_map/ppermute | solution.py:27
  29.3 1.4 %collective-permute-start.11 = (bf16[8,1,16,128]{3,2,1,0:T(8,128)(2,1)S(1)}, bf16[8,1,16,128]{3,2,1,0:T(8,128)(2,1)S(1)}, u32[]{:S(2)}, u32[]{:S(2)}) collective-permute-start(bf16[8,1,16,128]{3,2,1,0:T(8,128)(2,1)S(1)} %get-tuple-element.9), channel_id=1, source_target_pairs={{0,4},{4,0},{1,5},{5,1},{2,6},{6,2},{3,7},{7,3},{8,12},{12,8},{9,1... | collective-permute-start | bytes 98312 | tf_op jit(solution)/shard_map/ppermute | solution.py:203
